TPU v7x, 128 devices: a whole 4x4x4 slice. The times are simulated.
128 devices in a mesh: gx: 16 (over z, y), gy: 8 (over x, core).
Axes of the slice: x: 4, y: 4, z: 4, core: 2. Of those that a mesh axis runs over, the one named last changes fastest.
Arguments:
- multipole: bfloat16 [16384, 3, 296], P(('gx', 'gy')), may hold values from -6 to 6
- m2m_ops: bfloat16 [8, 296, 296], replicated, may hold values from -0.125 to 0.125
- m2l_ops: bfloat16 [64, 296, 296], replicated, may hold values from -0.09375 to 0.09375
- leaf_targets: int32 [128, 64, 80], P(('gx', 'gy')), may hold values from -1 to 16383, as said below
- leaf_sources: int32 [128, 64, 80], P(('gx', 'gy')), may hold values from -1 to 16383, as said below
- parent_targets: int32 [128, 64, 32], P(('gx', 'gy')), may hold values from -1 to 2047, as said below
- parent_sources: int32 [128, 64, 32], P(('gx', 'gy')), may hold values from -1 to 2047, as said below
Outputs:
- leaf_local: float32 [16384, 3, 296], P(('gx', 'gy'))
- parent_local: float32 [2048, 3, 296], P(('gx', 'gy'))
Inputs may be any that keep to these rules, and one draw needn't show every extreme that they name: Leaf box g belongs to device g // 128 of the combined axis gx+gy. An entry held at index d names target and source boxes of devices d - 2 to d + 2 (within the axis). A slot holds -1 in leaf_targets exactly when it holds -1 in leaf_sources. On every device some class has all 80 slots live. `leaf_sources`: same layout and reach as leaf_targets; -1 exactly in the same slots. `parent_targets`: parent box q belongs to device q // 16. An entry held at index d names target and source parents of devices d - 2 to d + 2. A slot holds -1 here exactly when it holds -1 in parent_sources. On every device some class has all 32 slots live. `parent_sources`: same layout and reach as parent_targets; -1 exactly in the same slots.
All inputs are finite; a program needn't handle non-finite values.
Results may differ from a plain program's by a relative error of at most 0.011.
Values may be sent and summed in bfloat16 or wider, within the bound.
A program may use at most 128 MiB of HBM per device.

v0:
```python
import math

import jax
import jax.numpy as jnp
from jax import lax
from jax.sharding import PartitionSpec as P

P_SIZE = 296
REACH = 2


def passed_along(block, axis, distance):
    devices = range(lax.axis_size(axis))
    route = [(i - distance, i) for i in devices if i - distance in devices]
    return lax.ppermute(block, axis, route)


def translate(window, targets, sources, ops, base, rows_dev):
    window_rows = window.shape[0]
    width = ops.shape[2]
    classes = ops.shape[0]
    slots = targets.shape[2]
    group = math.gcd(classes, 8)
    flattened = window.reshape(window_rows, 3 * width)
    columns = lax.broadcasted_iota(jnp.int32, (1, 1, window_rows), 2)
    tgt_blocks = targets[0].reshape(classes // group, group, slots)
    src_blocks = sources[0].reshape(classes // group, group, slots)
    op_blocks = ops.reshape(classes // group, group, width, width)

    def one_block(total, item):
        tgt_block, src_block, op_block = item
        src_local = jnp.where(src_block >= 0, src_block - base, -1)
        src_onehot = (src_local[:, :, None] == columns).astype(jnp.bfloat16)
        picked = jnp.einsum(
            "gsw,wf->gsf", src_onehot, flattened, preferred_element_type=jnp.float32
        )
        picked = picked.astype(jnp.bfloat16).reshape(group, slots, 3, width)
        terms = jnp.einsum("gscp,gpr->gscr", picked, op_block, preferred_element_type=jnp.float32)
        terms = terms.reshape(group, slots, 3 * width)
        upper_part = terms.astype(jnp.bfloat16)
        lower_part = (terms - upper_part.astype(jnp.float32)).astype(jnp.bfloat16)
        tgt_local = jnp.where(tgt_block >= 0, tgt_block - base, -1)
        tgt_onehot = (tgt_local[:, :, None] == columns).astype(jnp.bfloat16)
        added = jnp.einsum(
            "gsw,gsf->wf", tgt_onehot, upper_part, preferred_element_type=jnp.float32
        )
        added = added + jnp.einsum(
            "gsw,gsf->wf", tgt_onehot, lower_part, preferred_element_type=jnp.float32
        )
        return (total + added, None)

    start_total = jnp.zeros((window_rows, 3 * width), jnp.float32)
    partial_sum, unused = lax.scan(one_block, start_total, (tgt_blocks, src_blocks, op_blocks))
    return partial_sum.astype(jnp.bfloat16).reshape(2 * REACH + 1, rows_dev, 3, width)


def on_device(
    multipole, m2m_ops, m2l_ops, leaf_targets, leaf_sources, parent_targets, parent_sources
):
    here = lax.axis_index(("gx", "gy"))
    box_dev = multipole.shape[0]
    par_dev = box_dev // 8
    grouped = multipole.reshape(par_dev, 8, 3, P_SIZE)
    parent_multipole = jnp.einsum(
        "qocp,opr->qcr", grouped, m2m_ops, preferred_element_type=jnp.float32
    ).astype(jnp.bfloat16)
    own = (multipole, parent_multipole)
    lower = []
    upper = []
    for step in range(1, REACH + 1):
        lower.append(passed_along((own[0], own[1]), ("gx", "gy"), step))
        upper.append(passed_along((own[0], own[1]), ("gx", "gy"), -step))
    ordered = list(reversed(lower)) + [own] + upper
    leaf_window = jnp.concatenate([piece[0] for piece in ordered], axis=0)
    parent_window = jnp.concatenate([piece[1] for piece in ordered], axis=0)
    leaf_parts = translate(
        leaf_window, leaf_targets, leaf_sources, m2l_ops, (here - REACH) * box_dev, box_dev
    )
    parent_parts = translate(
        parent_window, parent_targets, parent_sources, m2l_ops, (here - REACH) * par_dev, par_dev
    )
    leaf_local = leaf_parts[REACH].astype(jnp.float32)
    parent_local = parent_parts[REACH].astype(jnp.float32)
    for offset in range(1, REACH + 1):
        arrived = passed_along(
            (leaf_parts[REACH + offset], parent_parts[REACH + offset]), ("gx", "gy"), offset
        )
        leaf_local = leaf_local + arrived[0].astype(jnp.float32)
        parent_local = parent_local + arrived[1].astype(jnp.float32)
        arrived = passed_along(
            (leaf_parts[REACH - offset], parent_parts[REACH - offset]), ("gx", "gy"), -offset
        )
        leaf_local = leaf_local + arrived[0].astype(jnp.float32)
        parent_local = parent_local + arrived[1].astype(jnp.float32)
    return (leaf_local, parent_local)


def solution(mesh):
    return jax.shard_map(
        on_device,
        mesh=mesh,
        in_specs=(
            P(("gx", "gy"), None, None),
            P(),
            P(),
            P(("gx", "gy"), None, None),
            P(("gx", "gy"), None, None),
            P(("gx", "gy"), None, None),
            P(("gx", "gy"), None, None),
        ),
        out_specs=(P(("gx", "gy"), None, None), P(("gx", "gy"), None, None)),
        check_vma=False,
    )
```

profile of v0, /device:TPU:31, one launch (start us, length us, event | category | flops | bytes accessed | tf_op | source)
XLA Modules:
  0.0 394.5 jit_solution(5985155043623619020)
XLA Ops:
  2.7 3.1 collective-permute-start.8
  5.8 3.1 collective-permute-start
  8.9 4.2 %collective-permute-start.1 = (bf16[128,3,296]{0,2,1:T(8,128)(2,1)}, bf16[128,3,296]{0,2,1:T(8,128)(2,1)}, u32[]{:S(2)}, u32[]{:S(2)}) collective-permute-start(bf16[128,3,296]{0,2,1:T(8,128)(2,1)} %param.11), channel_id=1, source_target_pairs={{0,1},{1,2},{2,3},{3,4},{4,5},{5,6},{6,7},{7,8},{8,9},{9,10},{10,1... | collective-permute-start | bytes 681992 | tf_op jit(solution)/shard_map/ppermute | solution.py:15
  18.1 8.1 %collective-permute-start.9 = (bf16[16,3,296]{2,0,1:T(8,128)(2,1)S(1)}, bf16[16,3,296]{2,0,1:T(8,128)(2,1)S(1)}, u32[]{:S(2)}, u32[]{:S(2)}) collective-permute-start(bf16[16,3,296]{2,0,1:T(8,128)(2,1)S(1)} %fusion.38), channel_id=1, source_target_pairs={{0,1},{1,2},{2,3},{3,4},{4,5},{5,6},{6,7},{7,8},{8,9},{9,10},{10,1... | collective-permute-start | bytes 85256 | tf_op jit(solution)/shard_map/ppermute | solution.py:15
  29.2 8.1 %collective-permute-done.10 = bf16[16,3,296]{2,0,1:T(8,128)(2,1)S(1)} collective-permute-done((bf16[16,3,296]{2,0,1:T(8,128)(2,1)S(1)}, bf16[16,3,296]{2,0,1:T(8,128)(2,1)S(1)}, u32[]{:S(2)}, u32[]{:S(2)}) %collective-permute-start.10) | collective-permute-done | bytes 28448 | tf_op jit(solution)/shard_map/ppermute | solution.py:15
  39.3 7.0 %collective-permute-done.11 = bf16[16,3,296]{2,0,1:T(8,128)(2,1)S(1)} collective-permute-done((bf16[16,3,296]{2,0,1:T(8,128)(2,1)S(1)}, bf16[16,3,296]{2,0,1:T(8,128)(2,1)S(1)}, u32[]{:S(2)}, u32[]{:S(2)}) %collective-permute-start.11) | collective-permute-done | bytes 28448 | tf_op jit(solution)/shard_map/ppermute | solution.py:15
  46.6 65.4 %while.25 = (s32[]{:T(128)}, f32[80,888]{1,0:T(8,128)S(1)}, s32[8,8,32]{2,1,0:T(8,128)S(1)}, s32[]{:T(128)}, s32[8,8,32]{2,1,0:T(8,128)}, /*index=5*/bf16[80,888...) while((s32[]{:T(128)}, f32[80,888]{1,0:T(8,128)S(1)}, ...), condition=%wide.region_3.4_spmd.clone.clone, body=%wide.region_2.3_spmd.clone.clone.sunk | while | flops 245335680 | bytes 11288443 | solution.py:53
  114.5 7.6 %collective-permute-start.14 = (bf16[16,3,296]{2,1,0:T(4,128)(2,1)S(1)}, bf16[16,3,296]{2,1,0:T(4,128)(2,1)S(1)}, u32[]{:S(2)}, u32[]{:S(2)}) collective-permute-start(bf16[16,3,296]{2,1,0:T(4,128)(2,1)S(1)} %squeeze.45), channel_id=1, source_target_pairs={{0,2},{1,3},{2,4},{3,5},{4,6},{5,7},{6,8},{7,9},{8,10},{9,11},{10,... | collective-permute-start | bytes 85256 | tf_op jit(solution)/shard_map/ppermute | solution.py:15
  127.0 8.0 %collective-permute-start.12 = (bf16[16,3,296]{2,1,0:T(4,128)(2,1)S(1)}, bf16[16,3,296]{2,1,0:T(4,128)(2,1)S(1)}, u32[]{:S(2)}, u32[]{:S(2)}) collective-permute-start(bf16[16,3,296]{2,1,0:T(4,128)(2,1)S(1)} %squeeze.43), channel_id=1, source_target_pairs={{0,1},{1,2},{2,3},{3,4},{4,5},{5,6},{6,7},{7,8},{8,9},{9,10},{10,1... | collective-permute-start | bytes 85256 | tf_op jit(solution)/shard_map/ppermute | solution.py:15
  138.1 231.3 %while.24 = (s32[]{:T(128)}, f32[640,888]{0,1:T(8,128)}, s32[8,8,80]{2,1,0:T(8,128)}, s32[]{:T(128)}, s32[8,8,80]{2,1,0:T(8,128)}, /*index=5*/bf16[640,888]{0,1:...) while((s32[]{:T(128)}, f32[640,888]{0,1:T(8,128)}, ...), condition=%wide.region_1.2_spmd.clone.clone, body=%wide.region_0.1_spmd.clone.clone.sunk | while | flops 2525141760 | bytes 33355384 | solution.py:53
  138.9 2.4 fusion.65
  141.3 2.6 reshape.147
  143.9 3.3 fusion.66
  147.2 3.4 copy.38
  150.6 5.6 %reshape.148 = f32[8,80,888]{2,1,0:T(8,128)} reshape(f32[8,80,3,296]{3,2,1,0:T(4,128)} %copy.38) | data formatting | bytes 4546560 | tf_op jit(solution)/shard_map/while/body/eval_jaxpr/reshape | solution.py:39
  156.2 5.1 %fusion.67 = f32[640,888,1]{0,1,2:T(8,128)} fusion(f32[8,80,888]{2,1,0:T(8,128)} %reshape.148, s32[8,80]{1,0:T(8,128)S(1)} %get-tuple-element.314), kind=kOutput, calls=%fused_computation.7.clone.1 | convolution fusion | flops 730132480 | bytes 4549120 | tf_op jit(solution)/shard_map/while/body/eval_jaxpr/gsw,gsf->wf/dot_general | solution.py:47
  161.3 5.1 %fusion.68 = f32[640,888]{0,1:T(8,128)} fusion(f32[640,888,1]{0,1,2:T(8,128)} %fusion.67, f32[640,888]{0,1:T(8,128)} %get-tuple-element.334, pred[]{:T(512)S(6)} %compare.6, s32[8,80]{1,0:T(8,128)S(1)} %get-tuple-element.314, f32[8,80,888]{2,1,0:T(8,128)} %reshape.148), kind=kOutput, calls=%fused_computation.6.clone.1 | convolution fusion | flops 730132480 | bytes 9095681 | tf_op jit(solution)/shard_map/while/body/eval_jaxpr/gsw,gsf->wf/dot_general | solution.py:44
  167.2 2.4 fusion.65
  169.6 2.6 reshape.147
  172.2 3.3 fusion.66
  175.5 3.4 copy.38
  178.9 5.6 %reshape.148 = f32[8,80,888]{2,1,0:T(8,128)} reshape(f32[8,80,3,296]{3,2,1,0:T(4,128)} %copy.38) | data formatting | bytes 4546560 | tf_op jit(solution)/shard_map/while/body/eval_jaxpr/reshape | solution.py:39
  184.5 5.1 %fusion.67 = f32[640,888,1]{0,1,2:T(8,128)} fusion(f32[8,80,888]{2,1,0:T(8,128)} %reshape.148, s32[8,80]{1,0:T(8,128)S(1)} %get-tuple-element.314), kind=kOutput, calls=%fused_computation.7.clone.1 | convolution fusion | flops 730132480 | bytes 4549120 | tf_op jit(solution)/shard_map/while/body/eval_jaxpr/gsw,gsf->wf/dot_general | solution.py:47
  189.6 5.8 %fusion.68 = f32[640,888]{0,1:T(8,128)} fusion(f32[640,888,1]{0,1,2:T(8,128)} %fusion.67, f32[640,888]{0,1:T(8,128)} %get-tuple-element.334, pred[]{:T(512)S(6)} %compare.6, s32[8,80]{1,0:T(8,128)S(1)} %get-tuple-element.314, f32[8,80,888]{2,1,0:T(8,128)} %reshape.148), kind=kOutput, calls=%fused_computation.6.clone.1 | convolution fusion | flops 730132480 | bytes 9095681 | tf_op jit(solution)/shard_map/while/body/eval_jaxpr/gsw,gsf->wf/dot_general | solution.py:44
  196.2 2.4 fusion.65
  198.6 2.6 reshape.147
  201.2 3.3 fusion.66
  204.5 3.4 copy.38
  207.9 5.6 %reshape.148 = f32[8,80,888]{2,1,0:T(8,128)} reshape(f32[8,80,3,296]{3,2,1,0:T(4,128)} %copy.38) | data formatting | bytes 4546560 | tf_op jit(solution)/shard_map/while/body/eval_jaxpr/reshape | solution.py:39
  213.5 5.1 %fusion.67 = f32[640,888,1]{0,1,2:T(8,128)} fusion(f32[8,80,888]{2,1,0:T(8,128)} %reshape.148, s32[8,80]{1,0:T(8,128)S(1)} %get-tuple-element.314), kind=kOutput, calls=%fused_computation.7.clone.1 | convolution fusion | flops 730132480 | bytes 4549120 | tf_op jit(solution)/shard_map/while/body/eval_jaxpr/gsw,gsf->wf/dot_general | solution.py:47
  218.6 5.8 %fusion.68 = f32[640,888]{0,1:T(8,128)} fusion(f32[640,888,1]{0,1,2:T(8,128)} %fusion.67, f32[640,888]{0,1:T(8,128)} %get-tuple-element.334, pred[]{:T(512)S(6)} %compare.6, s32[8,80]{1,0:T(8,128)S(1)} %get-tuple-element.314, f32[8,80,888]{2,1,0:T(8,128)} %reshape.148), kind=kOutput, calls=%fused_computation.6.clone.1 | convolution fusion | flops 730132480 | bytes 9095681 | tf_op jit(solution)/shard_map/while/body/eval_jaxpr/gsw,gsf->wf/dot_general | solution.py:44
  227.6 2.6 reshape.147
  230.2 3.3 fusion.66
  233.5 3.4 copy.38
  236.9 5.6 %reshape.148 = f32[8,80,888]{2,1,0:T(8,128)} reshape(f32[8,80,3,296]{3,2,1,0:T(4,128)} %copy.38) | data formatting | bytes 4546560 | tf_op jit(solution)/shard_map/while/body/eval_jaxpr/reshape | solution.py:39
  242.5 5.1 %fusion.67 = f32[640,888,1]{0,1,2:T(8,128)} fusion(f32[8,80,888]{2,1,0:T(8,128)} %reshape.148, s32[8,80]{1,0:T(8,128)S(1)} %get-tuple-element.314), kind=kOutput, calls=%fused_computation.7.clone.1 | convolution fusion | flops 730132480 | bytes 4549120 | tf_op jit(solution)/shard_map/while/body/eval_jaxpr/gsw,gsf->wf/dot_general | solution.py:47
  247.6 5.8 %fusion.68 = f32[640,888]{0,1:T(8,128)} fusion(f32[640,888,1]{0,1,2:T(8,128)} %fusion.67, f32[640,888]{0,1:T(8,128)} %get-tuple-element.334, pred[]{:T(512)S(6)} %compare.6, s32[8,80]{1,0:T(8,128)S(1)} %get-tuple-element.314, f32[8,80,888]{2,1,0:T(8,128)} %reshape.148), kind=kOutput, calls=%fused_computation.6.clone.1 | convolution fusion | flops 730132480 | bytes 9095681 | tf_op jit(solution)/shard_map/while/body/eval_jaxpr/gsw,gsf->wf/dot_general | solution.py:44
  254.1 2.4 fusion.65
  256.6 2.6 reshape.147
  259.2 3.3 fusion.66
  262.5 3.4 copy.38
  265.9 5.6 %reshape.148 = f32[8,80,888]{2,1,0:T(8,128)} reshape(f32[8,80,3,296]{3,2,1,0:T(4,128)} %copy.38) | data formatting | bytes 4546560 | tf_op jit(solution)/shard_map/while/body/eval_jaxpr/reshape | solution.py:39
  271.5 5.1 %fusion.67 = f32[640,888,1]{0,1,2:T(8,128)} fusion(f32[8,80,888]{2,1,0:T(8,128)} %reshape.148, s32[8,80]{1,0:T(8,128)S(1)} %get-tuple-element.314), kind=kOutput, calls=%fused_computation.7.clone.1 | convolution fusion | flops 730132480 | bytes 4549120 | tf_op jit(solution)/shard_map/while/body/eval_jaxpr/gsw,gsf->wf/dot_general | solution.py:47
  276.6 5.8 %fusion.68 = f32[640,888]{0,1:T(8,128)} fusion(f32[640,888,1]{0,1,2:T(8,128)} %fusion.67, f32[640,888]{0,1:T(8,128)} %get-tuple-element.334, pred[]{:T(512)S(6)} %compare.6, s32[8,80]{1,0:T(8,128)S(1)} %get-tuple-element.314, f32[8,80,888]{2,1,0:T(8,128)} %reshape.148), kind=kOutput, calls=%fused_computation.6.clone.1 | convolution fusion | flops 730132480 | bytes 9095681 | tf_op jit(solution)/shard_map/while/body/eval_jaxpr/gsw,gsf->wf/dot_general | solution.py:44
  285.6 2.6 reshape.147
  288.2 3.3 fusion.66
  291.5 3.4 copy.38
  294.9 5.6 %reshape.148 = f32[8,80,888]{2,1,0:T(8,128)} reshape(f32[8,80,3,296]{3,2,1,0:T(4,128)} %copy.38) | data formatting | bytes 4546560 | tf_op jit(solution)/shard_map/while/body/eval_jaxpr/reshape | solution.py:39
  300.5 5.1 %fusion.67 = f32[640,888,1]{0,1,2:T(8,128)} fusion(f32[8,80,888]{2,1,0:T(8,128)} %reshape.148, s32[8,80]{1,0:T(8,128)S(1)} %get-tuple-element.314), kind=kOutput, calls=%fused_computation.7.clone.1 | convolution fusion | flops 730132480 | bytes 4549120 | tf_op jit(solution)/shard_map/while/body/eval_jaxpr/gsw,gsf->wf/dot_general | solution.py:47
  305.6 5.8 %fusion.68 = f32[640,888]{0,1:T(8,128)} fusion(f32[640,888,1]{0,1,2:T(8,128)} %fusion.67, f32[640,888]{0,1:T(8,128)} %get-tuple-element.334, pred[]{:T(512)S(6)} %compare.6, s32[8,80]{1,0:T(8,128)S(1)} %get-tuple-element.314, f32[8,80,888]{2,1,0:T(8,128)} %reshape.148), kind=kOutput, calls=%fused_computation.6.clone.1 | convolution fusion | flops 730132480 | bytes 9095681 | tf_op jit(solution)/shard_map/while/body/eval_jaxpr/gsw,gsf->wf/dot_general | solution.py:44
  314.6 2.6 reshape.147
  317.2 3.3 fusion.66
  320.4 3.4 copy.38
  323.8 5.6 %reshape.148 = f32[8,80,888]{2,1,0:T(8,128)} reshape(f32[8,80,3,296]{3,2,1,0:T(4,128)} %copy.38) | data formatting | bytes 4546560 | tf_op jit(solution)/shard_map/while/body/eval_jaxpr/reshape | solution.py:39
  329.5 5.1 %fusion.67 = f32[640,888,1]{0,1,2:T(8,128)} fusion(f32[8,80,888]{2,1,0:T(8,128)} %reshape.148, s32[8,80]{1,0:T(8,128)S(1)} %get-tuple-element.314), kind=kOutput, calls=%fused_computation.7.clone.1 | convolution fusion | flops 730132480 | bytes 4549120 | tf_op jit(solution)/shard_map/while/body/eval_jaxpr/gsw,gsf->wf/dot_general | solution.py:47
  334.6 5.8 %fusion.68 = f32[640,888]{0,1:T(8,128)} fusion(f32[640,888,1]{0,1,2:T(8,128)} %fusion.67, f32[640,888]{0,1:T(8,128)} %get-tuple-element.334, pred[]{:T(512)S(6)} %compare.6, s32[8,80]{1,0:T(8,128)S(1)} %get-tuple-element.314, f32[8,80,888]{2,1,0:T(8,128)} %reshape.148), kind=kOutput, calls=%fused_computation.6.clone.1 | convolution fusion | flops 730132480 | bytes 9095681 | tf_op jit(solution)/shard_map/while/body/eval_jaxpr/gsw,gsf->wf/dot_general | solution.py:44
  343.6 2.6 reshape.147
  346.2 3.3 fusion.66
  349.5 3.4 copy.38
  352.8 5.6 %reshape.148 = f32[8,80,888]{2,1,0:T(8,128)} reshape(f32[8,80,3,296]{3,2,1,0:T(4,128)} %copy.38) | data formatting | bytes 4546560 | tf_op jit(solution)/shard_map/while/body/eval_jaxpr/reshape | solution.py:39
  358.5 5.1 %fusion.67 = f32[640,888,1]{0,1,2:T(8,128)} fusion(f32[8,80,888]{2,1,0:T(8,128)} %reshape.148, s32[8,80]{1,0:T(8,128)S(1)} %get-tuple-element.314), kind=kOutput, calls=%fused_computation.7.clone.1 | convolution fusion | flops 730132480 | bytes 4549120 | tf_op jit(solution)/shard_map/while/body/eval_jaxpr/gsw,gsf->wf/dot_general | solution.py:47
  363.6 5.8 %fusion.68 = f32[640,888]{0,1:T(8,128)} fusion(f32[640,888,1]{0,1,2:T(8,128)} %fusion.67, f32[640,888]{0,1:T(8,128)} %get-tuple-element.334, pred[]{:T(512)S(6)} %compare.6, s32[8,80]{1,0:T(8,128)S(1)} %get-tuple-element.314, f32[8,80,888]{2,1,0:T(8,128)} %reshape.148), kind=kOutput, calls=%fused_computation.6.clone.1 | convolution fusion | flops 730132480 | bytes 9095681 | tf_op jit(solution)/shard_map/while/body/eval_jaxpr/gsw,gsf->wf/dot_general | solution.py:44
  373.3 7.6 %collective-permute-start.6 = (bf16[128,3,296]{0,2,1:T(8,128)(2,1)S(1)}, bf16[128,3,296]{0,2,1:T(8,128)(2,1)S(1)}, u32[]{:S(2)}, u32[]{:S(2)}) collective-permute-start(bf16[128,3,296]{0,2,1:T(8,128)(2,1)S(1)} %bitcast.90), channel_id=1, source_target_pairs={{0,2},{1,3},{2,4},{3,5},{4,6},{5,7},{6,8},{7,9},{8,10},{9,11},{10,... | collective-permute-start | bytes 681992 | tf_op jit(solution)/shard_map/ppermute | solution.py:15
  382.9 7.9 %collective-permute-start.4 = (bf16[128,3,296]{0,2,1:T(8,128)(2,1)S(1)}, bf16[128,3,296]{0,2,1:T(8,128)(2,1)S(1)}, u32[]{:S(2)}, u32[]{:S(2)}) collective-permute-start(bf16[128,3,296]{0,2,1:T(8,128)(2,1)S(1)} %bitcast.88), channel_id=1, source_target_pairs={{0,1},{1,2},{2,3},{3,4},{4,5},{5,6},{6,7},{7,8},{8,9},{9,10},{10,1... | collective-permute-start | bytes 681992 | tf_op jit(solution)/shard_map/ppermute | solution.py:15
  (136 shorter events, 112.4 us)
Async XLA Ops:
  0.6 1.6 copy-start
  0.6 16.7 %copy-start.2 = (s32[1,64,32]{1,2,0:T(8,128)S(1)}, s32[1,64,32]{1,2,0:T(8,128)}, u32[]{:S(2)}) copy-start(s32[1,64,32]{1,2,0:T(8,128)} %param.16) | copy-start | bytes 24580
  0.7 16.7 %copy-start.3 = (s32[1,64,32]{1,2,0:T(8,128)S(1)}, s32[1,64,32]{1,2,0:T(8,128)}, u32[]{:S(2)}) copy-start(s32[1,64,32]{1,2,0:T(8,128)} %param.17) | copy-start | bytes 24580
  2.7 15.4 %collective-permute-start.8 = (bf16[16,3,296]{2,0,1:T(8,128)(2,1)S(1)}, bf16[16,3,296]{2,0,1:T(8,128)(2,1)S(1)}, u32[]{:S(2)}, u32[]{:S(2)}) collective-permute-start(bf16[16,3,296]{2,0,1:T(8,128)(2,1)S(1)} %fusion.38), channel_id=1, source_target_pairs={{0,2},{1,3},{2,4},{3,5},{4,6},{5,7},{6,8},{7,9},{8,10},{9,11},{10,... | collective-permute-start | bytes 85256 | tf_op jit(solution)/shard_map/ppermute | solution.py:15
  5.8 108.7 %collective-permute-start = (bf16[128,3,296]{0,2,1:T(8,128)(2,1)}, bf16[128,3,296]{0,2,1:T(8,128)(2,1)}, u32[]{:S(2)}, u32[]{:S(2)}) collective-permute-start(bf16[128,3,296]{0,2,1:T(8,128)(2,1)} %param.11), channel_id=1, source_target_pairs={{0,2},{1,3},{2,4},{3,5},{4,6},{5,7},{6,8},{7,9},{8,10},{9,11},{10,... | collective-permute-start | bytes 681992 | tf_op jit(solution)/shard_map/ppermute | solution.py:15
  8.9 114.2 %collective-permute-start.1 = (bf16[128,3,296]{0,2,1:T(8,128)(2,1)}, bf16[128,3,296]{0,2,1:T(8,128)(2,1)}, u32[]{:S(2)}, u32[]{:S(2)}) collective-permute-start(bf16[128,3,296]{0,2,1:T(8,128)(2,1)} %param.11), channel_id=1, source_target_pairs={{0,1},{1,2},{2,3},{3,4},{4,5},{5,6},{6,7},{7,8},{8,9},{9,10},{10,1... | collective-permute-start | bytes 681992 | tf_op jit(solution)/shard_map/ppermute | solution.py:15
  13.2 113.8 %collective-permute-start.2 = (bf16[128,3,296]{0,2,1:T(8,128)(2,1)}, bf16[128,3,296]{0,2,1:T(8,128)(2,1)}, u32[]{:S(2)}, u32[]{:S(2)}) collective-permute-start(bf16[128,3,296]{0,2,1:T(8,128)(2,1)} %param.11), channel_id=1, source_target_pairs={{1,0},{2,1},{3,2},{4,3},{5,4},{6,5},{7,6},{8,7},{9,8},{10,9},{11,1... | collective-permute-start | bytes 681992 | tf_op jit(solution)/shard_map/ppermute | solution.py:15
  15.1 121.0 %collective-permute-start.3 = (bf16[128,3,296]{0,2,1:T(8,128)(2,1)}, bf16[128,3,296]{0,2,1:T(8,128)(2,1)}, u32[]{:S(2)}, u32[]{:S(2)}) collective-permute-start(bf16[128,3,296]{0,2,1:T(8,128)(2,1)} %param.11), channel_id=1, source_target_pairs={{2,0},{3,1},{4,2},{5,3},{6,4},{7,5},{8,6},{9,7},{10,8},{11,9},{12,... | collective-permute-start | bytes 681992 | tf_op jit(solution)/shard_map/ppermute | solution.py:15
  18.1 9.2 %collective-permute-start.9 = (bf16[16,3,296]{2,0,1:T(8,128)(2,1)S(1)}, bf16[16,3,296]{2,0,1:T(8,128)(2,1)S(1)}, u32[]{:S(2)}, u32[]{:S(2)}) collective-permute-start(bf16[16,3,296]{2,0,1:T(8,128)(2,1)S(1)} %fusion.38), channel_id=1, source_target_pairs={{0,1},{1,2},{2,3},{3,4},{4,5},{5,6},{6,7},{7,8},{8,9},{9,10},{10,1... | collective-permute-start | bytes 85256 | tf_op jit(solution)/shard_map/ppermute | solution.py:15
  27.3 10.1 %collective-permute-start.10 = (bf16[16,3,296]{2,0,1:T(8,128)(2,1)S(1)}, bf16[16,3,296]{2,0,1:T(8,128)(2,1)S(1)}, u32[]{:S(2)}, u32[]{:S(2)}) collective-permute-start(bf16[16,3,296]{2,0,1:T(8,128)(2,1)S(1)} %fusion.38), channel_id=1, source_target_pairs={{1,0},{2,1},{3,2},{4,3},{5,4},{6,5},{7,6},{8,7},{9,8},{10,9},{11,1... | collective-permute-start | bytes 85256 | tf_op jit(solution)/shard_map/ppermute | solution.py:15
  37.4 8.9 %collective-permute-start.11 = (bf16[16,3,296]{2,0,1:T(8,128)(2,1)S(1)}, bf16[16,3,296]{2,0,1:T(8,128)(2,1)S(1)}, u32[]{:S(2)}, u32[]{:S(2)}) collective-permute-start(bf16[16,3,296]{2,0,1:T(8,128)(2,1)S(1)} %fusion.38), channel_id=1, source_target_pairs={{2,0},{3,1},{4,2},{5,3},{6,4},{7,5},{8,6},{9,7},{10,8},{11,9},{12,... | collective-permute-start | bytes 85256 | tf_op jit(solution)/shard_map/ppermute | solution.py:15
  112.1 261.2 %collective-permute-start.15 = (bf16[16,3,296]{2,1,0:T(4,128)(2,1)S(1)}, bf16[16,3,296]{2,1,0:T(4,128)(2,1)S(1)}, u32[]{:S(2)}, u32[]{:S(2)}) collective-permute-start(bf16[16,3,296]{2,1,0:T(4,128)(2,1)S(1)} %squeeze.46), channel_id=1, source_target_pairs={{2,0},{3,1},{4,2},{5,3},{6,4},{7,5},{8,6},{9,7},{10,8},{11,9},{12,... | collective-permute-start | bytes 85256 | tf_op jit(solution)/shard_map/ppermute | solution.py:15
  114.5 266.4 %collective-permute-start.14 = (bf16[16,3,296]{2,1,0:T(4,128)(2,1)S(1)}, bf16[16,3,296]{2,1,0:T(4,128)(2,1)S(1)}, u32[]{:S(2)}, u32[]{:S(2)}) collective-permute-start(bf16[16,3,296]{2,1,0:T(4,128)(2,1)S(1)} %squeeze.45), channel_id=1, source_target_pairs={{0,2},{1,3},{2,4},{3,5},{4,6},{5,7},{6,8},{7,9},{8,10},{9,11},{10,... | collective-permute-start | bytes 85256 | tf_op jit(solution)/shard_map/ppermute | solution.py:15
  123.1 259.8 %collective-permute-start.13 = (bf16[16,3,296]{2,1,0:T(4,128)(2,1)S(1)}, bf16[16,3,296]{2,1,0:T(4,128)(2,1)S(1)}, u32[]{:S(2)}, u32[]{:S(2)}) collective-permute-start(bf16[16,3,296]{2,1,0:T(4,128)(2,1)S(1)} %squeeze.44), channel_id=1, source_target_pairs={{1,0},{2,1},{3,2},{4,3},{5,4},{6,5},{7,6},{8,7},{9,8},{10,9},{11,1... | collective-permute-start | bytes 85256 | tf_op jit(solution)/shard_map/ppermute | solution.py:15
  127.0 263.7 %collective-permute-start.12 = (bf16[16,3,296]{2,1,0:T(4,128)(2,1)S(1)}, bf16[16,3,296]{2,1,0:T(4,128)(2,1)S(1)}, u32[]{:S(2)}, u32[]{:S(2)}) collective-permute-start(bf16[16,3,296]{2,1,0:T(4,128)(2,1)S(1)} %squeeze.43), channel_id=1, source_target_pairs={{0,1},{1,2},{2,3},{3,4},{4,5},{5,6},{6,7},{7,8},{8,9},{9,10},{10,1... | collective-permute-start | bytes 85256 | tf_op jit(solution)/shard_map/ppermute | solution.py:15
  137.1 1.1 copy-start.1
  371.4 20.1 %collective-permute-start.7 = (bf16[128,3,296]{0,2,1:T(8,128)(2,1)S(1)}, bf16[128,3,296]{0,2,1:T(8,128)(2,1)S(1)}, u32[]{:S(2)}, u32[]{:S(2)}) collective-permute-start(bf16[128,3,296]{0,2,1:T(8,128)(2,1)S(1)} %bitcast.91), channel_id=1, source_target_pairs={{2,0},{3,1},{4,2},{5,3},{6,4},{7,5},{8,6},{9,7},{10,8},{11,9},{12,... | collective-permute-start | bytes 681992 | tf_op jit(solution)/shard_map/ppermute | solution.py:15
  373.3 18.1 %collective-permute-start.6 = (bf16[128,3,296]{0,2,1:T(8,128)(2,1)S(1)}, bf16[128,3,296]{0,2,1:T(8,128)(2,1)S(1)}, u32[]{:S(2)}, u32[]{:S(2)}) collective-permute-start(bf16[128,3,296]{0,2,1:T(8,128)(2,1)S(1)} %bitcast.90), channel_id=1, source_target_pairs={{0,2},{1,3},{2,4},{3,5},{4,6},{5,7},{6,8},{7,9},{8,10},{9,11},{10,... | collective-permute-start | bytes 681992 | tf_op jit(solution)/shard_map/ppermute | solution.py:15
  380.9 11.5 %collective-permute-start.5 = (bf16[128,3,296]{0,2,1:T(8,128)(2,1)S(1)}, bf16[128,3,296]{0,2,1:T(8,128)(2,1)S(1)}, u32[]{:S(2)}, u32[]{:S(2)}) collective-permute-start(bf16[128,3,296]{0,2,1:T(8,128)(2,1)S(1)} %bitcast.89), channel_id=1, source_target_pairs={{1,0},{2,1},{3,2},{4,3},{5,4},{6,5},{7,6},{8,7},{9,8},{10,9},{11,1... | collective-permute-start | bytes 681992 | tf_op jit(solution)/shard_map/ppermute | solution.py:15
  382.9 10.8 %collective-permute-start.4 = (bf16[128,3,296]{0,2,1:T(8,128)(2,1)S(1)}, bf16[128,3,296]{0,2,1:T(8,128)(2,1)S(1)}, u32[]{:S(2)}, u32[]{:S(2)}) collective-permute-start(bf16[128,3,296]{0,2,1:T(8,128)(2,1)S(1)} %bitcast.88), channel_id=1, source_target_pairs={{0,1},{1,2},{2,3},{3,4},{4,5},{5,6},{6,7},{7,8},{8,9},{9,10},{10,1... | collective-permute-start | bytes 681992 | tf_op jit(solution)/shard_map/ppermute | solution.py:15
where the time goes:
time: 402 us; the launch traced here: 395 us
  matrix products  157 us (39%)
  local copies, waits for them, and re-layouts  138 us (34%)
  starting transfers between devices  65.3 us (16%)
  waiting for transfers between devices  18.4 us (5%)
  other arithmetic  14 us (3%)
    ppermute x16, starting transfers between devices, passed_along(): return lax.ppermute(block, axis, route)  65.3 us
    reshape x16, local copies, waits for them, and re-layouts, one_block(): terms = terms.reshape(group, slots, 3 * width)  59.8 us
    dot_general x16, matrix products, one_block(): jnp.einsum('gsw,gsf->wf', tgt_onehot, upper_part, preferred_element_type=...  48.4 us
    dot_general x16, matrix products, one_block(): jnp.einsum('gsw,gsf->wf', tgt_onehot, lower_part, preferred_element_type=...  43.8 us
    dot_general x16, local copies, waits for them, and re-layouts, one_block(): jnp.einsum('gscp,gpr->gscr', picked, op_block, preferred_element_type=jnp...  43 us
    dot_general x16, matrix products, one_block(): jnp.einsum('gscp,gpr->gscr', picked, op_block, preferred_element_type=jnp...  42.7 us
    reshape x16, local copies, waits for them, and re-layouts, one_block(): picked = picked.astype(jnp.bfloat16).reshape(group, slots, 3, width)  24.9 us
    dot_general x16, matrix products, one_block(): jnp.einsum('gsw,wf->gsf', src_onehot, flattened, preferred_element_type=j...  22.1 us
  transfers between devices with their start and end apart: 16, of which 5 were waited for; matrix products, arithmetic and copies ran while one was open for 77% of the time, Pallas kernels for 0%

commit v1 on v0

v1 whole, which is shorter than its diff:
```python
import functools

import jax
import jax.numpy as jnp
from jax import lax
from jax.experimental import pallas as pl
from jax.experimental.pallas import tpu as pltpu
from jax.sharding import PartitionSpec as P

CLASSES = 64
SLOT = 80
PSLOT = 32
SLOTS = SLOT + PSLOT
P_SIZE = 296
BOX_DEV = 128
PAR_DEV = 16
SPAN = 5
LEAVES = SPAN * BOX_DEV
ROWS = LEAVES + SPAN * PAR_DEV
ACC_ROWS = ROWS + 8
CHAINS = 4
DEVICES = 128
N_GY = 8
MESH = pl.DeviceIdType.MESH
f32 = jnp.float32
bf16 = jnp.bfloat16
OFFSETS = (1, -1, 2, -2)


def dot_nt(a, b):
    return lax.dot_general(a, b, (((1,), (1,)), ((), ())), preferred_element_type=f32)


def here():
    return lax.axis_index("gx") * N_GY + lax.axis_index("gy")


def neighbour(offset):
    index = lax.rem(here() + (offset + DEVICES), DEVICES)
    return (lax.div(index, N_GY), lax.rem(index, N_GY))


def entry_barrier():
    barrier = pltpu.get_barrier_semaphore()
    for offset in OFFSETS:
        pl.semaphore_signal(barrier, inc=1, device_id=neighbour(offset), device_id_type=MESH)
    pl.semaphore_wait(barrier, len(OFFSETS))


def slot_of(offset):
    j = 2 - offset
    return j if j < 2 else j - 1


def exchange_kernel(
    mp, m2m, lt, ls, pt, ps, rem, par, idx, own, ops, par_own, send, recv, psend, precv, local
):
    get_own = pltpu.make_async_copy(mp, own, local.at[0])
    get_ops = pltpu.make_async_copy(m2m, ops, local.at[1])
    get_own.start()
    get_ops.start()
    entry_barrier()
    leaf_copies = []
    for n, offset in enumerate(OFFSETS):
        copy = pltpu.make_async_remote_copy(
            src_ref=mp,
            dst_ref=rem.at[slot_of(offset)],
            send_sem=send.at[n],
            recv_sem=recv.at[n],
            device_id=neighbour(offset),
            device_id_type=MESH,
        )
        copy.start()
        leaf_copies.append(copy)

    row = lax.broadcasted_iota(jnp.int32, (128, 128), 0)
    column = lax.broadcasted_iota(jnp.int32, (128, 128), 1)
    wanted = 8 * lax.rem(row, 16) + lax.div(row, 16)
    select = (column == wanted).astype(f32).astype(bf16)
    get_own.wait()
    by_octant = [dot_nt(select, own[c]).astype(bf16) for c in range(3)]
    get_ops.wait()
    total = jnp.zeros((48, P_SIZE), f32)
    for o in range(8):
        rows = jnp.concatenate([by_octant[c][16 * o : 16 * o + 16] for c in range(3)], axis=0)
        total = total + jnp.dot(rows, ops[o], preferred_element_type=f32)
    pieces = []
    for c in range(3):
        part = total[16 * c : 16 * c + 16]
        for q in range(2):
            par_own[2 * c + q] = part[:, 128 * q : 128 * q + 128].astype(bf16)
        pieces.append(
            jnp.concatenate([part[:, 256:296], jnp.zeros((16, 88), f32)], axis=1)
        )
    tails = pieces[0] + pltpu.roll(pieces[1], 40, 1) + pltpu.roll(pieces[2], 80, 1)
    par_own[6] = tails.astype(bf16)
    keep = pltpu.make_async_copy(par_own, par.at[2], local.at[2])
    keep.start()
    par_copies = []
    for n, offset in enumerate(OFFSETS):
        copy = pltpu.make_async_remote_copy(
            src_ref=par_own,
            dst_ref=par.at[2 - offset],
            send_sem=psend.at[n],
            recv_sem=precv.at[n],
            device_id=neighbour(offset),
            device_id_type=MESH,
        )
        copy.start()
        par_copies.append(copy)

    leaf_base = (here() - 2) * BOX_DEV
    par_base = (here() - 2) * PAR_DEV - LEAVES
    idx[...] = jnp.zeros_like(idx)
    idx[0, 0:64, 0:80] = jnp.where(ls[...] >= 0, ls[...] - leaf_base, 0)
    idx[1, 0:64, 0:80] = jnp.where(lt[...] >= 0, lt[...] - leaf_base, ROWS)
    idx[0, 64:96, 0:64] = jnp.where(ps[...] >= 0, ps[...] - par_base, 0)
    idx[1, 64:96, 0:64] = jnp.where(pt[...] >= 0, pt[...] - par_base, ROWS)

    keep.wait()
    for copy in leaf_copies + par_copies:
        copy.wait()


def translate_kernel(idx, mp, rem, par, ops_hbm, out, win, g, o0, o1, g1, ops, sem, *acc):
    gathered, terms = (g, g1), (o0, o1)

    def fetch(k):
        return pltpu.make_async_copy(ops_hbm.at[k], ops.at[k], sem.at[k])

    @pl.loop(0, CLASSES)
    def _(k):
        fetch(k).start()

    row = lax.broadcasted_iota(jnp.int32, (128, 128), 0)
    column = lax.broadcasted_iota(jnp.int32, (128, 128), 1)
    eye = (row == column).astype(f32).astype(bf16)
    for j in range(SPAN):
        src = mp if j == 2 else rem.at[j if j < 2 else j - 1]
        for c in range(3):
            m = dot_nt(eye, src[c, 0:256, :])
            for q in range(2):
                win[pl.ds(j * 1024 + 2 * c + q, 128, stride=8), :] = m[:, 128 * q : 128 * q + 128]
        tails = jnp.concatenate(
            [src[c, 256:296, :] for c in range(3)] + [jnp.zeros((8, 128), bf16)], axis=0
        )
        win[pl.ds(j * 1024 + 6, 128, stride=8), :] = dot_nt(eye, tails)
        for r in range(7):
            win[pl.ds((LEAVES + j * 16) * 8 + r, 16, stride=8), :] = par[j, r].astype(f32)
    zeros = jnp.zeros((64, 128), f32)
    for buffer in (o0, o1):

        @pl.loop(0, SLOTS // 8)
        def _(i):
            buffer[pl.ds(pl.multiple_of(i * 64, 64), 64), :] = zeros

    for a in acc:

        @pl.loop(0, ACC_ROWS // 8)
        def _(i):
            a[pl.ds(pl.multiple_of(i * 64, 64), 64), :] = zeros

    def at(which, k, s):
        place = idx[which, k, s] if s < SLOT else idx[which, 64 + s - SLOT, k]
        return pl.ds(pl.multiple_of(place * 8, 8), 8)

    def gather(k, b):
        for s in range(SLOTS):
            gathered[b][s * 8 : s * 8 + 8, :] = win[at(0, k, s), :]

    def scatter(k, b):
        for s in range(SLOTS):
            acc[s % CHAINS][at(1, k, s), :] += terms[b][s * 8 : s * 8 + 8, :]

    def multiply(k, b):
        rows = [gathered[b][pl.ds(r, SLOTS, stride=8), :] for r in range(7)]
        tails = (rows[6], pltpu.roll(rows[6], 88, 1), pltpu.roll(rows[6], 48, 1))
        x = jnp.concatenate(
            [
                jnp.concatenate(
                    [
                        rows[2 * c].astype(bf16),
                        rows[2 * c + 1].astype(bf16),
                        tails[c].astype(bf16)[:, :40],
                    ],
                    axis=1,
                )
                for c in range(3)
            ],
            axis=0,
        )
        y = jnp.dot(x, ops[k], preferred_element_type=f32)
        pieces = []
        for c in range(3):
            part = y[c * SLOTS : (c + 1) * SLOTS]
            for q in range(2):
                terms[b][pl.ds(2 * c + q, SLOTS, stride=8), :] = part[:, 128 * q : 128 * q + 128]
            pieces.append(
                jnp.concatenate([part[:, 256:296], jnp.zeros((SLOTS, 88), f32)], axis=1)
            )
        terms[b][pl.ds(6, SLOTS, stride=8), :] = (
            pieces[0] + pltpu.roll(pieces[1], 40, 1) + pltpu.roll(pieces[2], 80, 1)
        )

    gather(0, 0)

    @pl.loop(0, CLASSES // 2)
    def _(i):
        k = 2 * i
        fetch(k).wait()
        fetch(k + 1).wait()
        gather(k + 1, 1)
        multiply(k, 0)
        scatter(jnp.maximum(k - 1, 0), 1)
        gather(jnp.minimum(k + 2, CLASSES - 1), 0)
        multiply(k + 1, 1)
        scatter(k, 0)

    scatter(CLASSES - 1, 1)

    def total(start, count):
        rows = pl.ds(start, count, stride=8)
        return functools.reduce(lambda p, q: p + q, [a[rows, :] for a in acc])

    for j in range(SPAN):
        for r in range(7):
            leaf = total(j * 1024 + r, 128).astype(bf16)
            out[j, r, 0:128, :] = dot_nt(eye, leaf).astype(bf16)
            out[j, r, 128:144, :] = total(LEAVES * 8 + j * 128 + r, 16).astype(bf16)


def sum_kernel(partial, leaf, parent, own, got, send, recv, local):
    get_own = pltpu.make_async_copy(partial.at[2], own, local)
    get_own.start()
    entry_barrier()
    copies = []
    for n, offset in enumerate(OFFSETS):
        copy = pltpu.make_async_remote_copy(
            src_ref=partial.at[2 + offset],
            dst_ref=got.at[n],
            send_sem=send.at[n],
            recv_sem=recv.at[n],
            device_id=neighbour(offset),
            device_id_type=MESH,
        )
        copy.start()
        copies.append(copy)
    get_own.wait()
    for copy in copies:
        copy.wait()

    def total(r):
        s = own[r].astype(f32)
        for n in range(4):
            s = s + got[n, r].astype(f32)
        return s

    for c in range(3):
        for q in range(2):
            s = total(2 * c + q)
            leaf[c, 128 * q : 128 * q + 128, :] = s[0:128]
            parent[c, :, 128 * q : 128 * q + 128] = s[128:144]
    s = total(6)
    for c in range(3):
        leaf[c, 256:296, :] = s[40 * c : 40 * c + 40]
        shifted = s[128:144] if c == 0 else pltpu.roll(s[128:144], 128 - 40 * c, 1)
        parent[c, :, 256:296] = shifted[:, :40]


def on_device(multipole, m2m_ops, m2l_ops, lt, ls, pt, ps):
    mp = jnp.transpose(multipole, (1, 2, 0))
    pt, ps = jnp.transpose(pt[0]), jnp.transpose(ps[0])
    vmem = pl.BlockSpec(memory_space=pltpu.VMEM)
    smem = pl.BlockSpec(memory_space=pltpu.SMEM)
    anywhere = pl.BlockSpec(memory_space=pl.ANY)
    rem, par, idx = pl.pallas_call(
        exchange_kernel,
        out_shape=(
            jax.ShapeDtypeStruct((4, 3, P_SIZE, BOX_DEV), bf16),
            jax.ShapeDtypeStruct((SPAN, 7, PAR_DEV, 128), bf16),
            jax.ShapeDtypeStruct((2, 104, 128), jnp.int32),
        ),
        in_specs=[anywhere, anywhere, vmem, vmem, vmem, vmem],
        out_specs=(anywhere, anywhere, vmem),
        scratch_shapes=[
            pltpu.VMEM((3, P_SIZE, BOX_DEV), bf16),
            pltpu.VMEM((8, P_SIZE, P_SIZE), bf16),
            pltpu.VMEM((7, PAR_DEV, 128), bf16),
            pltpu.SemaphoreType.DMA((4,)),
            pltpu.SemaphoreType.DMA((4,)),
            pltpu.SemaphoreType.DMA((4,)),
            pltpu.SemaphoreType.DMA((4,)),
            pltpu.SemaphoreType.DMA((3,)),
        ],
        compiler_params=pltpu.CompilerParams(
            collective_id=0, has_side_effects=True, vmem_limit_bytes=32 * 1024 * 1024
        ),
        name="exchange",
    )(mp, m2m_ops, lt[0], ls[0], pt, ps)
    partial = pl.pallas_call(
        translate_kernel,
        out_shape=jax.ShapeDtypeStruct((SPAN, 7, BOX_DEV + PAR_DEV, 128), bf16),
        in_specs=[smem, vmem, vmem, vmem, anywhere],
        out_specs=vmem,
        scratch_shapes=[pltpu.VMEM((ACC_ROWS * 8, 128), f32)]
        + [pltpu.VMEM((SLOTS * 8, 128), f32)] * 4
        + [pltpu.VMEM((CLASSES, P_SIZE, P_SIZE), bf16), pltpu.SemaphoreType.DMA((CLASSES,))]
        + [pltpu.VMEM((ACC_ROWS * 8, 128), f32)] * CHAINS,
        compiler_params=pltpu.CompilerParams(vmem_limit_bytes=56 * 1024 * 1024),
        name="translate",
    )(idx, mp, rem, par, m2l_ops)
    leaf, parent = pl.pallas_call(
        sum_kernel,
        out_shape=(
            jax.ShapeDtypeStruct((3, P_SIZE, BOX_DEV), f32),
            jax.ShapeDtypeStruct((3, PAR_DEV, P_SIZE), f32),
        ),
        in_specs=[anywhere],
        out_specs=(vmem, vmem),
        scratch_shapes=[
            pltpu.VMEM((7, BOX_DEV + PAR_DEV, 128), bf16),
            pltpu.VMEM((4, 7, BOX_DEV + PAR_DEV, 128), bf16),
            pltpu.SemaphoreType.DMA((4,)),
            pltpu.SemaphoreType.DMA((4,)),
            pltpu.SemaphoreType.DMA,
        ],
        compiler_params=pltpu.CompilerParams(
            collective_id=1, has_side_effects=True, vmem_limit_bytes=32 * 1024 * 1024
        ),
        name="sums",
    )(partial)
    return jnp.transpose(leaf, (2, 0, 1)), jnp.transpose(parent, (1, 0, 2))


def solution(mesh):
    boxes = P(("gx", "gy"), None, None)
    return jax.shard_map(
        on_device,
        mesh=mesh,
        in_specs=(boxes, P(), P(), boxes, boxes, boxes, boxes),
        out_specs=(boxes, boxes),
        check_vma=False,
    )
```

time: 402 us -> 84 us (0.21)
  the two profiles are of different devices: /device:TPU:31 before, /device:TPU:1 now
where the time goes in v1:
time: 84 us; the launch traced here: 83.5 us
  Pallas kernels  72.6 us (86%)
  local copies, waits for them, and re-layouts  10.3 us (12%)
    pallas_call x1, Pallas kernels, on_device(): pl.pallas_call(translate_kernel, out_shape=jax.ShapeDtypeStruct((SPAN, 7,...  35.8 us
    pallas_call x1, Pallas kernels, on_device(): pl.pallas_call(exchange_kernel, out_shape=(jax.ShapeDtypeStruct((4, 3, P_...  20 us
    pallas_call x1, Pallas kernels, on_device(): pl.pallas_call(sum_kernel, out_shape=(jax.ShapeDtypeStruct((3, P_SIZE, BO...  16.8 us
    unnamed x22, local copies, waits for them, and re-layouts  10.3 us

profile of v1, /device:TPU:1, one launch (start us, length us, event | category | flops | bytes accessed | tf_op | source)
XLA Modules:
  0.0 83.5 jit_solution(10342978202426484741)
XLA Ops:
  0.6 0.0 copy-start.1
  0.6 1.5 %copy-done.1 = bf16[8,296,296]{2,1,0:T(8,128)(2,1)S(1)} copy-done((bf16[8,296,296]{2,1,0:T(8,128)(2,1)S(1)}, bf16[8,296,296]{2,1,0:T(8,128)(2,1)}, u32[]{:S(2)}) %copy-start.1) | copy-done | bytes 1401880
  2.1 0.0 copy-start.3
  2.1 0.9 %copy-done.3 = bf16[128,3,296]{0,2,1:T(8,128)(2,1)S(1)} copy-done((bf16[128,3,296]{0,2,1:T(8,128)(2,1)S(1)}, bf16[128,3,296]{0,2,1:T(8,128)(2,1)}, u32[]{:S(2)}) %copy-start.3) | copy-done | bytes 227352
  3.1 0.0 copy-start.6
  3.1 0.8 copy-done.6
  3.8 0.0 copy-start.7
  3.8 0.8 copy-done.7
  4.6 0.0 copy-start.8
  4.6 0.7 copy-done.8
  5.3 0.0 copy-start.9
  5.3 0.7 copy-done.9
  6.0 20.0 %exchange.1 = (bf16[4,3,296,128]{3,2,1,0:T(8,128)(2,1)S(1)}, bf16[5,7,16,128]{3,2,1,0:T(8,128)(2,1)S(1)}, s32[2,104,128]{2,1,0:T(8,128)S(1)}) custom-call(bf16[3,296,128]{2,1,0:T(8,128)(2,1)S(1)} %bitcast.12, bf16[8,296,296]{2,1,0:T(8,128)(2,1)S(1)} %copy-done.1, s32[64,80]{1,0:T(8,128)S(1)} %bitcast.15, s32[64,80]{1,0:T(8,128)S(1)} %bitcast.16, ...), custom_call_target="tpu_custom_call" | custom-call | tf_op jit(solution)/shard_map/exchange/pallas_call | solution.py:276
  26.0 0.0 copy-start.2
  26.0 0.9 %copy-done.2 = bf16[4,3,296,128]{3,2,1,0:T(8,128)(2,1)} copy-done((bf16[4,3,296,128]{3,2,1,0:T(8,128)(2,1)}, bf16[4,3,296,128]{3,2,1,0:T(8,128)(2,1)S(1)}, u32[]{:S(2)}) %copy-start.2) | copy-done | bytes 909336
  26.9 0.0 copy-start.4
  26.9 0.7 copy-done.4
  27.6 0.0 copy-start.5
  27.6 0.6 copy-done.5
  28.2 35.8 %translate.1.partial = bf16[5,7,144,128]{3,2,1,0:T(8,128)(2,1)} custom-call(s32[2,104,128]{2,1,0:T(8,128)} %copy-done.5, bf16[3,296,128]{2,1,0:T(8,128)(2,1)} %bitcast.11, bf16[4,3,296,128]{3,2,1,0:T(8,128)(2,1)} %copy-done.2, bf16[5,7,16,128]{3,2,1,0:T(8,128)(2,1)} %copy-done.4, bf16[64,296,296]{2,1,0:T(8,128)(2,1)} %ops_hbm.1), custom_call_target="tpu_custom_call" | custom-call | tf_op jit(solution)/shard_map/translate/pallas_call | solution.py:300
  64.0 0.0 copy-start
  64.0 1.3 %copy-done = bf16[5,7,144,128]{3,2,1,0:T(8,128)(2,1)S(1)} copy-done((bf16[5,7,144,128]{3,2,1,0:T(8,128)(2,1)S(1)}, bf16[5,7,144,128]{3,2,1,0:T(8,128)(2,1)}, u32[]{:S(2)}) %copy-start) | copy-done | bytes 1290264
  65.3 16.8 %sums.1 = (f32[3,296,128]{2,1,0:T(8,128)S(1)}, f32[3,16,296]{2,1,0:T(8,128)S(1)}) custom-call(bf16[5,7,144,128]{3,2,1,0:T(8,128)(2,1)S(1)} %copy-done), custom_call_target="tpu_custom_call" | custom-call | tf_op jit(solution)/shard_map/sums/pallas_call | solution.py:312
  82.1 0.8 copy.11
  82.9 0.6 copy.12
Async XLA Ops:
  0.6 1.5 %copy-start.1 = (bf16[8,296,296]{2,1,0:T(8,128)(2,1)S(1)}, bf16[8,296,296]{2,1,0:T(8,128)(2,1)}, u32[]{:S(2)}) copy-start(bf16[8,296,296]{2,1,0:T(8,128)(2,1)} %m2m.1) | copy-start | bytes 4205572
  2.1 0.9 %copy-start.3 = (bf16[128,3,296]{0,2,1:T(8,128)(2,1)S(1)}, bf16[128,3,296]{0,2,1:T(8,128)(2,1)}, u32[]{:S(2)}) copy-start(bf16[128,3,296]{0,2,1:T(8,128)(2,1)} %param.7) | copy-start | bytes 681988
  3.1 0.8 copy-start.6
  3.8 0.8 copy-start.7
  4.6 0.7 copy-start.8
  5.3 0.7 copy-start.9
  26.0 0.9 %copy-start.2 = (bf16[4,3,296,128]{3,2,1,0:T(8,128)(2,1)}, bf16[4,3,296,128]{3,2,1,0:T(8,128)(2,1)S(1)}, u32[]{:S(2)}) copy-start(bf16[4,3,296,128]{3,2,1,0:T(8,128)(2,1)S(1)} %get-tuple-element.8.rem) | copy-start | bytes 2727940
  26.9 0.7 copy-start.4
  27.6 0.6 copy-start.5
  64.0 1.3 %copy-start = (bf16[5,7,144,128]{3,2,1,0:T(8,128)(2,1)S(1)}, bf16[5,7,144,128]{3,2,1,0:T(8,128)(2,1)}, u32[]{:S(2)}) copy-start(bf16[5,7,144,128]{3,2,1,0:T(8,128)(2,1)} %translate.1.partial) | copy-start | bytes 3870724

commit v2 on v1

v2 whole, which is shorter than its diff:
```python
import functools

import jax
import jax.numpy as jnp
from jax import lax
from jax.experimental import pallas as pl
from jax.experimental.pallas import tpu as pltpu
from jax.sharding import PartitionSpec as P

CLASSES = 64
SLOT = 80
PSLOT = 32
BUCKETS = (3, 4, 5, 6, 7)
SLOTS = SLOT + PSLOT
P_SIZE = 296
BOX_DEV = 128
PAR_DEV = 16
SPAN = 5
LEAVES = SPAN * BOX_DEV
ROWS = LEAVES + SPAN * PAR_DEV
ACC_ROWS = ROWS + 8
CHAINS = 4
DEVICES = 128
VMEM_BYTES = 63 * 1024 * 1024
N_GY = 8
MESH = pl.DeviceIdType.MESH
f32 = jnp.float32
bf16 = jnp.bfloat16
OFFSETS = (1, -1, 2, -2)


def dot_nt(a, b):
    return lax.dot_general(a, b, (((1,), (1,)), ((), ())), preferred_element_type=f32)


def mask16(x):
    return x.astype(f32).astype(bf16)


def iota(shape, dim):
    return lax.broadcasted_iota(jnp.int32, shape, dim)


def here():
    return lax.axis_index("gx") * N_GY + lax.axis_index("gy")


def neighbour(offset):
    index = lax.rem(here() + (offset + DEVICES), DEVICES)
    return (lax.div(index, N_GY), lax.rem(index, N_GY))


def entry_barrier():
    barrier = pltpu.get_barrier_semaphore()
    for offset in OFFSETS:
        pl.semaphore_signal(barrier, inc=1, device_id=neighbour(offset), device_id_type=MESH)
    pl.semaphore_wait(barrier, len(OFFSETS))


def slot_of(offset):
    j = 2 - offset
    return j if j < 2 else j - 1


def prepare_lists(ls, lt, ps, pt, leaf_base, par_base, values, place, packed, idx):
    eye = mask16(iota((64, 64), 0) == iota((64, 64), 1))

    def together(leaf, parent):
        low = jnp.concatenate(
            [jnp.zeros((80, 64), bf16), mask16(parent), jnp.zeros((16, 64), bf16)], axis=0
        )
        high = jnp.concatenate([leaf.astype(f32), jnp.zeros((64, 48), f32)], axis=1)
        return high + dot_nt(eye, low)

    leaf_live, par_live = ls[...] >= 0, ps[...] >= 0
    sl = jnp.where(leaf_live, ls[...] - leaf_base, 0)
    tl = jnp.where(leaf_live, lt[...] - leaf_base, 0)
    sp = jnp.where(par_live, ps[...] - par_base, 0)
    tp = jnp.where(par_live, pt[...] - par_base, 0)
    parts = [
        together(sl >> 3, sp >> 3),
        together(sl & 7, sp & 7),
        together(tl >> 3, tp >> 3),
        together(tl & 7, tp & 7),
        together(leaf_live, par_live),
    ]
    live = parts[4].astype(bf16)
    earlier = mask16(iota((128, 128), 0) < iota((128, 128), 1))
    before = jnp.dot(live, earlier, preferred_element_type=f32)
    place[...] = jnp.where(parts[4] > 0.5, before, 200.0)
    values[...] = jnp.zeros_like(values)
    for q, part in enumerate(parts):
        values[pl.ds(q, 64, stride=8), :] = part
    wanted = iota((128, 128), 0).astype(f32)

    @pl.loop(0, CLASSES, unroll=16)
    def _(k):
        hit = mask16(wanted == place[pl.ds(k, 1), :])
        rows = pl.ds(pl.multiple_of(k * 8, 8), 8)
        packed[rows, :] = dot_nt(values[rows, :].astype(bf16), hit)

    ones = jnp.ones((128, 128), bf16)
    count = jnp.dot(live, ones, preferred_element_type=f32)
    count_row = dot_nt(ones[0:16], live)[0:1, :]
    row, column = iota((64, 64), 0), iota((64, 64), 1)
    count_column = count[:, 0:64]
    ahead = mask16(
        (count_row < count_column) | ((count_row == count_column) & (column < row))
    )
    rank = dot_nt(ones[0:16, 0:64], ahead)[0:1, :]
    perm = mask16(rank == row.astype(f32))

    def sort(v):
        return jnp.dot(perm, v.astype(bf16), preferred_element_type=f32)

    s_high, s_low, t_high, t_low, used = (
        sort(packed[pl.ds(q, 64, stride=8), :]) for q in range(5)
    )
    order = sort(iota((64, 128), 0).astype(f32))
    lane = iota((64, 128), 1)
    source = (s_high * 8 + s_low) * 8
    target = jnp.where(used > 0.5, t_high * 8 + t_low, float(ROWS)) * 8
    idx[0, 0:64, :] = jnp.where(lane == 120, order, source).astype(jnp.int32)
    idx[1, 0:64, :] = target.astype(jnp.int32)
    fits = mask16(count <= (16 * lane).astype(f32))
    pairs = jnp.dot(ones[0:16, 0:64], fits, preferred_element_type=f32)[0:8]
    idx[0, 64:72, :] = pairs.astype(jnp.int32) >> 1
    idx[1, 64:72, :] = jnp.zeros((8, 128), jnp.int32)


def exchange_kernel(
    mp, m2m, lt_in, ls_in, pt_in, ps_in, rem, par, idx_out,
    own, ops, par_own, lt, ls, pt, ps, values, place, packed, idx,
    send, recv, psend, precv, local,
):
    staged = [
        pltpu.make_async_copy(src, dst, local.at[n])
        for n, (src, dst) in enumerate(
            ((mp, own), (m2m, ops), (lt_in, lt), (ls_in, ls), (pt_in, pt), (ps_in, ps))
        )
    ]
    for copy in staged:
        copy.start()
    entry_barrier()
    leaf_copies = []
    for n, offset in enumerate(OFFSETS):
        copy = pltpu.make_async_remote_copy(
            src_ref=mp,
            dst_ref=rem.at[slot_of(offset)],
            send_sem=send.at[n],
            recv_sem=recv.at[n],
            device_id=neighbour(offset),
            device_id_type=MESH,
        )
        copy.start()
        leaf_copies.append(copy)
    for copy in staged:
        copy.wait()

    row = iota((128, 128), 0)
    select = mask16(iota((128, 128), 1) == 8 * (row & 15) + (row >> 4))
    by_octant = [dot_nt(select, own[c]).astype(bf16) for c in range(3)]
    total = jnp.zeros((48, P_SIZE), f32)
    for o in range(8):
        rows = jnp.concatenate([by_octant[c][16 * o : 16 * o + 16] for c in range(3)], axis=0)
        total = total + jnp.dot(rows, ops[o], preferred_element_type=f32)
    pieces = []
    for c in range(3):
        part = total[16 * c : 16 * c + 16]
        for q in range(2):
            par_own[2 * c + q] = part[:, 128 * q : 128 * q + 128].astype(bf16)
        pieces.append(jnp.concatenate([part[:, 256:296], jnp.zeros((16, 88), f32)], axis=1))
    tails = pieces[0] + pltpu.roll(pieces[1], 40, 1) + pltpu.roll(pieces[2], 80, 1)
    par_own[6] = tails.astype(bf16)
    keep = pltpu.make_async_copy(par_own, par.at[2], local.at[6])
    keep.start()
    par_copies = []
    for n, offset in enumerate(OFFSETS):
        copy = pltpu.make_async_remote_copy(
            src_ref=par_own,
            dst_ref=par.at[2 - offset],
            send_sem=psend.at[n],
            recv_sem=precv.at[n],
            device_id=neighbour(offset),
            device_id_type=MESH,
        )
        copy.start()
        par_copies.append(copy)

    leaf_base = (here() - 2) * BOX_DEV
    par_base = (here() - 2) * PAR_DEV - LEAVES
    prepare_lists(ls, lt, ps, pt, leaf_base, par_base, values, place, packed, idx)
    put = pltpu.make_async_copy(idx, idx_out, local.at[7])
    put.start()

    keep.wait()
    put.wait()
    for copy in leaf_copies + par_copies:
        copy.wait()


def translate_kernel(
    idx_in, mp, rem, par_in, ops_in, out,
    idx, blocks, par, result, win, g0, g1, o0, o1, ops, ops_sem, sem, *acc,
):
    gathered, terms = (g0, g1), (o0, o1)
    get_idx = pltpu.make_async_copy(idx_in, idx, sem.at[0])
    get_idx.start()
    get_blocks = []
    for j in range(SPAN):
        src = mp if j == 2 else rem.at[j if j < 2 else j - 1]
        get_blocks.append(pltpu.make_async_copy(src, blocks.at[j], sem.at[1 + j]))
        get_blocks[j].start()
    get_par = pltpu.make_async_copy(par_in, par, sem.at[6])
    get_par.start()

    zeros = jnp.zeros((448, 128), f32)
    for a in acc:

        @pl.loop(0, ACC_ROWS * 8 // 448)
        def _(i):
            a[pl.ds(pl.multiple_of(i * 448, 448), 448), :] = zeros

    for buffer in terms:
        buffer[...] = jnp.zeros_like(buffer)

    get_idx.wait()

    def fetch(r):
        return pltpu.make_async_copy(ops_in.at[idx[0, r, 120]], ops.at[r], ops_sem.at[r])

    @pl.loop(0, CLASSES)
    def _(r):
        fetch(r).start()

    eye = mask16(iota((128, 128), 0) == iota((128, 128), 1))
    get_par.wait()
    for j in range(SPAN):
        get_blocks[j].wait()
        for c in range(3):
            m = dot_nt(eye, blocks[j, c, 0:256, :])
            for q in range(2):
                win[pl.ds(j * 1024 + 2 * c + q, 128, stride=8), :] = m[:, 128 * q : 128 * q + 128]
        tails = jnp.concatenate(
            [blocks[j, c, 256:296, :] for c in range(3)] + [jnp.zeros((8, 128), bf16)], axis=0
        )
        win[pl.ds(j * 1024 + 6, 128, stride=8), :] = dot_nt(eye, tails)
        for r in range(7):
            win[pl.ds((LEAVES + j * 16) * 8 + r, 16, stride=8), :] = par[j, r].astype(f32)

    def at(which, k, s):
        return pl.ds(pl.multiple_of(idx[which, k, s], 8), 8)

    def gather(k, b, n):
        for s in range(n):
            gathered[b][s * 8 : s * 8 + 8, :] = win[at(0, k, s), :]

    def scatter(k, b, n):
        for s in range(n):
            acc[s % CHAINS][at(1, k, s), :] += terms[b][s * 8 : s * 8 + 8, :]

    def multiply(k, b, n):
        rows = [gathered[b][pl.ds(r, n, stride=8), :] for r in range(7)]
        tails = (rows[6], pltpu.roll(rows[6], 88, 1), pltpu.roll(rows[6], 48, 1))
        x = jnp.concatenate(
            [
                jnp.concatenate(
                    [
                        rows[2 * c].astype(bf16),
                        rows[2 * c + 1].astype(bf16),
                        tails[c].astype(bf16)[:, :40],
                    ],
                    axis=1,
                )
                for c in range(3)
            ],
            axis=0,
        )
        y = jnp.dot(x, ops[k], preferred_element_type=f32)
        pieces = []
        for c in range(3):
            part = y[c * n : (c + 1) * n]
            for q in range(2):
                terms[b][pl.ds(2 * c + q, n, stride=8), :] = part[:, 128 * q : 128 * q + 128]
            pieces.append(jnp.concatenate([part[:, 256:296], jnp.zeros((n, 88), f32)], axis=1))
        terms[b][pl.ds(6, n, stride=8), :] = (
            pieces[0] + pltpu.roll(pieces[1], 40, 1) + pltpu.roll(pieces[2], 80, 1)
        )

    start = 0
    for bucket in BUCKETS:
        n = 16 * bucket
        end = idx[0, 64, bucket]

        @pl.when(end > start)
        def _():
            gather(2 * start, 0, n)

        @pl.loop(start, end)
        def _(i):
            k = 2 * i
            fetch(k).wait()
            fetch(k + 1).wait()
            gather(k + 1, 1, n)
            multiply(k, 0, n)
            scatter(jnp.maximum(k - 1, 0), 1, n)
            gather(jnp.minimum(k + 2, CLASSES - 1), 0, n)
            multiply(k + 1, 1, n)
            scatter(k, 0, n)

        start = end
    scatter(CLASSES - 1, 1, SLOTS)

    def total(first, count):
        rows = pl.ds(first, count, stride=8)
        return functools.reduce(lambda p, q: p + q, [a[rows, :] for a in acc])

    puts = []
    for j in range(SPAN):
        for r in range(7):
            leaf = total(j * 1024 + r, 128).astype(bf16)
            result[j, r, 0:128, :] = dot_nt(eye, leaf).astype(bf16)
            result[j, r, 128:144, :] = total(LEAVES * 8 + j * 128 + r, 16).astype(bf16)
        puts.append(pltpu.make_async_copy(result.at[j], out.at[j], sem.at[7 + j]))
        puts[j].start()
    for put in puts:
        put.wait()


def sum_kernel(partial, leaf, parent, own, got, send, recv, local):
    get_own = pltpu.make_async_copy(partial.at[2], own, local)
    get_own.start()
    entry_barrier()
    copies = []
    for n, offset in enumerate(OFFSETS):
        copy = pltpu.make_async_remote_copy(
            src_ref=partial.at[2 + offset],
            dst_ref=got.at[n],
            send_sem=send.at[n],
            recv_sem=recv.at[n],
            device_id=neighbour(offset),
            device_id_type=MESH,
        )
        copy.start()
        copies.append(copy)
    get_own.wait()
    for copy in copies:
        copy.wait()

    def total(r):
        s = own[r].astype(f32)
        for n in range(4):
            s = s + got[n, r].astype(f32)
        return s

    for c in range(3):
        for q in range(2):
            s = total(2 * c + q)
            leaf[c, 128 * q : 128 * q + 128, :] = s[0:128]
            parent[c, :, 128 * q : 128 * q + 128] = s[128:144]
    s = total(6)
    for c in range(3):
        leaf[c, 256:296, :] = s[40 * c : 40 * c + 40]
        shifted = s[128:144] if c == 0 else pltpu.roll(s[128:144], 128 - 40 * c, 1)
        parent[c, :, 256:296] = shifted[:, :40]


def on_device(multipole, m2m_ops, m2l_ops, lt, ls, pt, ps):
    mp = jnp.transpose(multipole, (1, 2, 0))
    pt, ps = jnp.transpose(pt[0]), jnp.transpose(ps[0])
    vmem = pl.BlockSpec(memory_space=pltpu.VMEM)
    hbm = pl.BlockSpec(memory_space=pltpu.HBM)
    semaphores = pltpu.SemaphoreType.DMA
    rem, par, idx = pl.pallas_call(
        exchange_kernel,
        out_shape=(
            jax.ShapeDtypeStruct((4, 3, P_SIZE, BOX_DEV), bf16),
            jax.ShapeDtypeStruct((SPAN, 7, PAR_DEV, 128), bf16),
            jax.ShapeDtypeStruct((2, 72, 128), jnp.int32),
        ),
        in_specs=[hbm] * 6,
        out_specs=(hbm, hbm, hbm),
        scratch_shapes=[
            pltpu.VMEM((3, P_SIZE, BOX_DEV), bf16),
            pltpu.VMEM((8, P_SIZE, P_SIZE), bf16),
            pltpu.VMEM((7, PAR_DEV, 128), bf16),
            pltpu.VMEM((CLASSES, SLOT), jnp.int32),
            pltpu.VMEM((CLASSES, SLOT), jnp.int32),
            pltpu.VMEM((PSLOT, CLASSES), jnp.int32),
            pltpu.VMEM((PSLOT, CLASSES), jnp.int32),
            pltpu.VMEM((CLASSES * 8, 128), f32),
            pltpu.VMEM((CLASSES, 128), f32),
            pltpu.VMEM((CLASSES * 8, 128), f32),
            pltpu.VMEM((2, 72, 128), jnp.int32),
            semaphores((4,)),
            semaphores((4,)),
            semaphores((4,)),
            semaphores((4,)),
            semaphores((8,)),
        ],
        compiler_params=pltpu.CompilerParams(
            collective_id=0, has_side_effects=True, vmem_limit_bytes=VMEM_BYTES
        ),
        name="exchange",
    )(mp, m2m_ops, lt[0], ls[0], pt, ps)
    partial = pl.pallas_call(
        translate_kernel,
        out_shape=jax.ShapeDtypeStruct((SPAN, 7, BOX_DEV + PAR_DEV, 128), bf16),
        in_specs=[hbm] * 5,
        out_specs=hbm,
        scratch_shapes=[
            pltpu.SMEM((2, 72, 128), jnp.int32),
            pltpu.VMEM((SPAN, 3, P_SIZE, BOX_DEV), bf16),
            pltpu.VMEM((SPAN, 7, PAR_DEV, 128), bf16),
            pltpu.VMEM((SPAN, 7, BOX_DEV + PAR_DEV, 128), bf16),
            pltpu.VMEM((ROWS * 8, 128), f32),
        ]
        + [pltpu.VMEM((SLOTS * 8, 128), f32)] * 4
        + [pltpu.VMEM((CLASSES, P_SIZE, P_SIZE), bf16), semaphores((CLASSES,)), semaphores((12,))]
        + [pltpu.VMEM((ACC_ROWS * 8, 128), f32)] * CHAINS,
        compiler_params=pltpu.CompilerParams(vmem_limit_bytes=VMEM_BYTES),
        name="translate",
    )(idx, mp, rem, par, m2l_ops)
    leaf, parent = pl.pallas_call(
        sum_kernel,
        out_shape=(
            jax.ShapeDtypeStruct((3, P_SIZE, BOX_DEV), f32),
            jax.ShapeDtypeStruct((3, PAR_DEV, P_SIZE), f32),
        ),
        in_specs=[hbm],
        out_specs=(vmem, vmem),
        scratch_shapes=[
            pltpu.VMEM((7, BOX_DEV + PAR_DEV, 128), bf16),
            pltpu.VMEM((4, 7, BOX_DEV + PAR_DEV, 128), bf16),
            semaphores((4,)),
            semaphores((4,)),
            semaphores,
        ],
        compiler_params=pltpu.CompilerParams(
            collective_id=1, has_side_effects=True, vmem_limit_bytes=VMEM_BYTES
        ),
        name="sums",
    )(partial)
    return jnp.transpose(leaf, (2, 0, 1)), jnp.transpose(parent, (1, 0, 2))


def solution(mesh):
    boxes = P(("gx", "gy"), None, None)
    return jax.shard_map(
        on_device,
        mesh=mesh,
        in_specs=(boxes, P(), P(), boxes, boxes, boxes, boxes),
        out_specs=(boxes, boxes),
        check_vma=False,
    )
```

time: 84 us -> 65.8 us (0.78)
  Pallas kernels: 72.6 us -> 61.5 us
  local copies, waits for them, and re-layouts: 10.3 us -> 3.33 us
    pallas_call x1, Pallas kernels: 35.8 us -> 24.3 us  [on_device(): pl.pallas_call(translate_kernel, out_shape=jax.ShapeDtypeStruct((SPAN, 7,...]
    unnamed x22 -> x2, local copies, waits for them, and re-layouts: 10.3 us -> 3.33 us
where the time goes in v2:
time: 65.8 us; the launch traced here: 65.5 us
  Pallas kernels  61.5 us (93%)
  local copies, waits for them, and re-layouts  3.33 us (5%)
  between operations  0.66 us (1%)
    pallas_call x1, Pallas kernels, on_device(): pl.pallas_call(translate_kernel, out_shape=jax.ShapeDtypeStruct((SPAN, 7,...  24.3 us
    pallas_call x1, Pallas kernels, on_device(): pl.pallas_call(exchange_kernel, out_shape=(jax.ShapeDtypeStruct((4, 3, P_...  19.6 us
    pallas_call x1, Pallas kernels, on_device(): pl.pallas_call(sum_kernel, out_shape=(jax.ShapeDtypeStruct((3, P_SIZE, BO...  17.6 us
    unnamed x2, local copies, waits for them, and re-layouts  3.33 us

profile of v2, /device:TPU:1, one launch (start us, length us, event | category | flops | bytes accessed | tf_op | source)
XLA Modules:
  0.0 65.5 jit_solution(16224786853820707081)
XLA Ops:
  0.6 19.6 %exchange.1 = (bf16[4,3,296,128]{3,2,1,0:T(8,128)(2,1)}, bf16[5,7,16,128]{3,2,1,0:T(8,128)(2,1)}, s32[2,72,128]{2,1,0:T(8,128)}) custom-call(bf16[3,296,128]{2,1,0:T(8,128)(2,1)} %bitcast.11, bf16[8,296,296]{2,1,0:T(8,128)(2,1)} %m2m.1, s32[64,80]{1,0:T(8,128)} %bitcast.15, s32[64,80]{1,0:T(8,128)} %bitcast.16, s32[32,64]{1,0:T(8,128)} %bitcast.17, ...), custom_call_target="tpu_custom_call" | custom-call | tf_op jit(solution)/shard_map/exchange/pallas_call | solution.py:374
  20.3 24.3 %translate.1.partial = bf16[5,7,144,128]{3,2,1,0:T(8,128)(2,1)} custom-call(s32[2,72,128]{2,1,0:T(8,128)} %get-tuple-element.7.idx_in, bf16[3,296,128]{2,1,0:T(8,128)(2,1)} %bitcast.12, bf16[4,3,296,128]{3,2,1,0:T(8,128)(2,1)} %get-tuple-element.8.rem, bf16[5,7,16,128]{3,2,1,0:T(8,128)(2,1)} %get-tuple-element.9.par_in, bf16[64,296,296]{2,1,0:T(8,128)(2,1)} %ops_in.1), custom_call_target="tpu_custom_call" | custom-call | tf_op jit(solution)/shard_map/translate/pallas_call | solution.py:406
  44.6 17.6 %sums.1 = (f32[3,296,128]{2,1,0:T(8,128)}, f32[3,16,296]{2,1,0:T(8,128)}) custom-call(bf16[5,7,144,128]{3,2,1,0:T(8,128)(2,1)} %translate.1.partial), custom_call_target="tpu_custom_call" | custom-call | tf_op jit(solution)/shard_map/sums/pallas_call | solution.py:424
  62.2 1.8 %copy.11 = f32[128,3,296]{0,2,1:T(8,128)} copy(f32[128,3,296]{0,2,1:T(8,128)} %bitcast.13) | data formatting | bytes 909312
  64.0 1.5 %copy.12 = f32[16,3,296]{2,0,1:T(8,128)} copy(f32[16,3,296]{2,0,1:T(8,128)} %bitcast.14) | data formatting | bytes 113664

commit v3 on v2

--- a/solution.py
+++ b/solution.py
@@ -26,7 +26,6 @@
 MESH = pl.DeviceIdType.MESH
 f32 = jnp.float32
 bf16 = jnp.bfloat16
-OFFSETS = (1, -1, 2, -2)
 
 
 def dot_nt(a, b):
@@ -45,21 +44,105 @@
     return lax.axis_index("gx") * N_GY + lax.axis_index("gy")
 
 
-def neighbour(offset):
+def device_at(offset):
     index = lax.rem(here() + (offset + DEVICES), DEVICES)
     return (lax.div(index, N_GY), lax.rem(index, N_GY))
 
 
+def sides():
+    me = here()
+    out = 2 * lax.rem(me, 2) - 1
+    ahead, behind = me + 2 * out, me - 2 * out
+    return out, (ahead >= 0) & (ahead < DEVICES), (behind >= 0) & (behind < DEVICES)
+
+
 def entry_barrier():
     barrier = pltpu.get_barrier_semaphore()
-    for offset in OFFSETS:
-        pl.semaphore_signal(barrier, inc=1, device_id=neighbour(offset), device_id_type=MESH)
-    pl.semaphore_wait(barrier, len(OFFSETS))
-
-
-def slot_of(offset):
-    j = 2 - offset
-    return j if j < 2 else j - 1
+    out, out_ok, in_ok = sides()
+
+    def greet(offset):
+        pl.semaphore_signal(barrier, inc=1, device_id=device_at(offset), device_id_type=MESH)
+
+    greet(-out)
+
+    @pl.when(out_ok)
+    def _():
+        greet(out)
+        greet(2 * out)
+
+    @pl.when(in_ok)
+    def _():
+        greet(-2 * out)
+
+    pl.semaphore_wait(barrier, 1 + 2 * out_ok.astype(jnp.int32) + in_ok.astype(jnp.int32))
+
+
+def remote(src, dst, send, recv, n, offset):
+    return pltpu.make_async_remote_copy(
+        src_ref=src,
+        dst_ref=dst,
+        send_sem=send.at[n],
+        recv_sem=recv.at[n],
+        device_id=device_at(offset),
+        device_id_type=MESH,
+    )
+
+
+class Spread:
+    def __init__(self, own, blocks, cut, send, recv):
+        out, self.out_ok, self.in_ok = sides()
+        first, rest = pl.ds(0, cut), pl.ds(cut, own.shape[0] - cut)
+        copy = functools.partial(remote, send=send, recv=recv)
+        self.sibling = copy(own, blocks.at[2 + out], n=0, offset=-out)
+        self.behind = copy(own, blocks.at[2 + 2 * out], n=1, offset=-2 * out)
+        self.near = copy(own.at[first], blocks.at[2 - out, first], n=2, offset=out)
+        self.far = copy(own.at[rest], blocks.at[2 - 2 * out, rest], n=3, offset=2 * out)
+        self.relay_near = copy(
+            blocks.at[2 + out, first], blocks.at[2 + 2 * out, first], n=4, offset=-out
+        )
+        self.relay_far = copy(
+            blocks.at[2 - 2 * out, rest], blocks.at[2 - out, rest], n=5, offset=-out
+        )
+
+    def start(self):
+        @pl.when(self.out_ok)
+        def _():
+            self.near.start()
+            self.far.start()
+
+        @pl.when(self.in_ok)
+        def _():
+            self.behind.start()
+
+        self.sibling.start()
+
+    def relay(self):
+        @pl.when(self.out_ok)
+        def _():
+            self.near.wait_recv()
+            self.relay_near.start()
+
+        @pl.when(self.in_ok)
+        def _():
+            self.far.wait_recv()
+            self.relay_far.start()
+
+    def finish(self):
+        self.sibling.wait()
+
+        @pl.when(self.out_ok)
+        def _():
+            self.near.wait_send()
+            self.far.wait_send()
+            self.behind.wait_recv()
+            self.relay_near.wait_send()
+            self.relay_far.wait_recv()
+
+        @pl.when(self.in_ok)
+        def _():
+            self.behind.wait_send()
+            self.relay_far.wait_send()
+            self.relay_near.wait_recv()
 
 
 def prepare_lists(ls, lt, ps, pt, leaf_base, par_base, values, place, packed, idx):
@@ -142,18 +225,8 @@
     for copy in staged:
         copy.start()
     entry_barrier()
-    leaf_copies = []
-    for n, offset in enumerate(OFFSETS):
-        copy = pltpu.make_async_remote_copy(
-            src_ref=mp,
-            dst_ref=rem.at[slot_of(offset)],
-            send_sem=send.at[n],
-            recv_sem=recv.at[n],
-            device_id=neighbour(offset),
-            device_id_type=MESH,
-        )
-        copy.start()
-        leaf_copies.append(copy)
+    leaves = Spread(mp, rem, 2, send, recv)
+    leaves.start()
     for copy in staged:
         copy.wait()
 
@@ -174,18 +247,8 @@
     par_own[6] = tails.astype(bf16)
     keep = pltpu.make_async_copy(par_own, par.at[2], local.at[6])
     keep.start()
-    par_copies = []
-    for n, offset in enumerate(OFFSETS):
-        copy = pltpu.make_async_remote_copy(
-            src_ref=par_own,
-            dst_ref=par.at[2 - offset],
-            send_sem=psend.at[n],
-            recv_sem=precv.at[n],
-            device_id=neighbour(offset),
-            device_id_type=MESH,
-        )
-        copy.start()
-        par_copies.append(copy)
+    parents = Spread(par_own, par, 4, psend, precv)
+    parents.start()
 
     leaf_base = (here() - 2) * BOX_DEV
     par_base = (here() - 2) * PAR_DEV - LEAVES
@@ -193,10 +256,12 @@
     put = pltpu.make_async_copy(idx, idx_out, local.at[7])
     put.start()
 
+    leaves.relay()
+    parents.relay()
     keep.wait()
     put.wait()
-    for copy in leaf_copies + par_copies:
-        copy.wait()
+    leaves.finish()
+    parents.finish()
 
 
 def translate_kernel(
@@ -208,7 +273,7 @@
     get_idx.start()
     get_blocks = []
     for j in range(SPAN):
-        src = mp if j == 2 else rem.at[j if j < 2 else j - 1]
+        src = mp if j == 2 else rem.at[j]
         get_blocks.append(pltpu.make_async_copy(src, blocks.at[j], sem.at[1 + j]))
         get_blocks[j].start()
     get_par = pltpu.make_async_copy(par_in, par, sem.at[6])
@@ -327,31 +392,87 @@
         put.wait()
 
 
-def sum_kernel(partial, leaf, parent, own, got, send, recv, local):
-    get_own = pltpu.make_async_copy(partial.at[2], own, local)
-    get_own.start()
+def sum_kernel(
+    partial, leaf, parent, own, mine_near, mine_far, from_near, from_far, side, behind, ahead,
+    send, recv, local,
+):
+    out, out_ok, in_ok = sides()
+    first, rest = pl.ds(0, 4), pl.ds(4, 3)
+    staged = [
+        pltpu.make_async_copy(src, dst, local.at[n])
+        for n, (src, dst) in enumerate(
+            (
+                (partial.at[2], own),
+                (partial.at[2 + out, first], mine_near),
+                (partial.at[2 - 2 * out, rest], mine_far),
+            )
+        )
+    ]
+    for copy in staged:
+        copy.start()
+    copy = functools.partial(remote, send=send, recv=recv)
+    lend_far = copy(partial.at[2 - 2 * out, first], from_near, n=0, offset=-out)
+    lend_near = copy(partial.at[2 + out, rest], from_far, n=1, offset=-out)
+    to_side = copy(partial.at[2 - out], side, n=2, offset=-out)
+    to_far = copy(partial.at[2 + 2 * out], behind, n=3, offset=2 * out)
+    sum_near = copy(mine_near, ahead.at[first], n=4, offset=out)
+    sum_far = copy(mine_far, ahead.at[rest], n=5, offset=-2 * out)
     entry_barrier()
-    copies = []
-    for n, offset in enumerate(OFFSETS):
-        copy = pltpu.make_async_remote_copy(
-            src_ref=partial.at[2 + offset],
-            dst_ref=got.at[n],
-            send_sem=send.at[n],
-            recv_sem=recv.at[n],
-            device_id=neighbour(offset),
-            device_id_type=MESH,
-        )
-        copy.start()
-        copies.append(copy)
-    get_own.wait()
-    for copy in copies:
-        copy.wait()
+
+    @pl.when(in_ok)
+    def _():
+        lend_far.start()
+
+    @pl.when(out_ok)
+    def _():
+        lend_near.start()
+        to_far.start()
+
+    to_side.start()
+    for c in staged:
+        c.wait()
+
+    def add(mine, theirs):
+        mine[...] = (mine[...].astype(f32) + theirs[...].astype(f32)).astype(bf16)
+
+    @pl.when(out_ok)
+    def _():
+        lend_far.wait_recv()
+        add(mine_near, from_near)
+        sum_near.start()
+
+    @pl.when(in_ok)
+    def _():
+        lend_near.wait_recv()
+        add(mine_far, from_far)
+        sum_far.start()
+
+    to_side.wait()
+
+    @pl.when(out_ok)
+    def _():
+        lend_near.wait_send()
+        to_far.wait_send()
+        sum_near.wait()
+        sum_far.wait_recv()
+
+    @pl.when(in_ok)
+    def _():
+        lend_far.wait_send()
+        to_far.wait_recv()
+        sum_far.wait_send()
+
+    @pl.when(jnp.logical_not(out_ok))
+    def _():
+        ahead[...] = jnp.zeros_like(ahead)
+
+    @pl.when(jnp.logical_not(in_ok))
+    def _():
+        behind[...] = jnp.zeros_like(behind)
 
     def total(r):
-        s = own[r].astype(f32)
-        for n in range(4):
-            s = s + got[n, r].astype(f32)
-        return s
+        s = own[r].astype(f32) + side[r].astype(f32)
+        return s + behind[r].astype(f32) + ahead[r].astype(f32)
 
     for c in range(3):
         for q in range(2):
@@ -365,6 +486,18 @@
         parent[c, :, 256:296] = shifted[:, :40]
 
 
+def write_kernel(leaf_in, parent_in, leaf, parent, sem):
+    copies = [
+        pltpu.make_async_copy(src.at[c], dst.at[c], sem.at[2 * c + n])
+        for c in range(3)
+        for n, (src, dst) in enumerate(((leaf_in, leaf), (parent_in, parent)))
+    ]
+    for copy in copies:
+        copy.start()
+    for copy in copies:
+        copy.wait()
+
+
 def on_device(multipole, m2m_ops, m2l_ops, lt, ls, pt, ps):
     mp = jnp.transpose(multipole, (1, 2, 0))
     pt, ps = jnp.transpose(pt[0]), jnp.transpose(ps[0])
@@ -374,7 +507,7 @@
     rem, par, idx = pl.pallas_call(
         exchange_kernel,
         out_shape=(
-            jax.ShapeDtypeStruct((4, 3, P_SIZE, BOX_DEV), bf16),
+            jax.ShapeDtypeStruct((SPAN, 3, P_SIZE, BOX_DEV), bf16),
             jax.ShapeDtypeStruct((SPAN, 7, PAR_DEV, 128), bf16),
             jax.ShapeDtypeStruct((2, 72, 128), jnp.int32),
         ),
@@ -392,10 +525,10 @@
             pltpu.VMEM((CLASSES, 128), f32),
             pltpu.VMEM((CLASSES * 8, 128), f32),
             pltpu.VMEM((2, 72, 128), jnp.int32),
-            semaphores((4,)),
-            semaphores((4,)),
-            semaphores((4,)),
-            semaphores((4,)),
+            semaphores((6,)),
+            semaphores((6,)),
+            semaphores((6,)),
+            semaphores((6,)),
             semaphores((8,)),
         ],
         compiler_params=pltpu.CompilerParams(
@@ -421,26 +554,43 @@
         compiler_params=pltpu.CompilerParams(vmem_limit_bytes=VMEM_BYTES),
         name="translate",
     )(idx, mp, rem, par, m2l_ops)
+    block = (7, BOX_DEV + PAR_DEV, 128)
+    results = (
+        jax.ShapeDtypeStruct((3, P_SIZE, BOX_DEV), f32),
+        jax.ShapeDtypeStruct((3, PAR_DEV, P_SIZE), f32),
+    )
     leaf, parent = pl.pallas_call(
         sum_kernel,
-        out_shape=(
-            jax.ShapeDtypeStruct((3, P_SIZE, BOX_DEV), f32),
-            jax.ShapeDtypeStruct((3, PAR_DEV, P_SIZE), f32),
-        ),
+        out_shape=results,
         in_specs=[hbm],
         out_specs=(vmem, vmem),
         scratch_shapes=[
-            pltpu.VMEM((7, BOX_DEV + PAR_DEV, 128), bf16),
-            pltpu.VMEM((4, 7, BOX_DEV + PAR_DEV, 128), bf16),
-            semaphores((4,)),
-            semaphores((4,)),
-            semaphores,
+            pltpu.VMEM(block, bf16),
+            pltpu.VMEM((4,) + block[1:], bf16),
+            pltpu.VMEM((3,) + block[1:], bf16),
+            pltpu.VMEM((4,) + block[1:], bf16),
+            pltpu.VMEM((3,) + block[1:], bf16),
+            pltpu.VMEM(block, bf16),
+            pltpu.VMEM(block, bf16),
+            pltpu.VMEM(block, bf16),
+            semaphores((6,)),
+            semaphores((6,)),
+            semaphores((3,)),
         ],
         compiler_params=pltpu.CompilerParams(
             collective_id=1, has_side_effects=True, vmem_limit_bytes=VMEM_BYTES
         ),
         name="sums",
     )(partial)
+    leaf, parent = pl.pallas_call(
+        write_kernel,
+        out_shape=results,
+        in_specs=[hbm, hbm],
+        out_specs=(hbm, hbm),
+        scratch_shapes=[semaphores((6,))],
+        compiler_params=pltpu.CompilerParams(vmem_limit_bytes=VMEM_BYTES),
+        name="write",
+    )(leaf, parent)
     return jnp.transpose(leaf, (2, 0, 1)), jnp.transpose(parent, (1, 0, 2))
 
 

time: 65.8 us -> 71 us (1.079)
  the two profiles are of different devices: /device:TPU:1 before, /device:TPU:31 now
where the time goes in v3:
time: 71 us; the launch traced here: 70.6 us
  Pallas kernels  70 us (99%)
    pallas_call x1, Pallas kernels, on_device(): pl.pallas_call(translate_kernel, out_shape=jax.ShapeDtypeStruct((SPAN, 7,...  24.2 us
    pallas_call x1, Pallas kernels, on_device(): pl.pallas_call(write_kernel, out_shape=results, in_specs=[hbm, hbm], out_...  17.2 us
    pallas_call x1, Pallas kernels, on_device(): pl.pallas_call(exchange_kernel, out_shape=(jax.ShapeDtypeStruct((SPAN, 3,...  14.5 us
    pallas_call x1, Pallas kernels, on_device(): pl.pallas_call(sum_kernel, out_shape=results, in_specs=[hbm], out_specs=(...  14.1 us

profile of v3, /device:TPU:31, one launch (start us, length us, event | category | flops | bytes accessed | tf_op | source)
XLA Modules:
  0.0 70.6 jit_solution(16375104108444206832)
XLA Ops:
  0.6 14.5 %exchange.1 = (bf16[5,3,296,128]{3,2,1,0:T(8,128)(2,1)}, bf16[5,7,16,128]{3,2,1,0:T(8,128)(2,1)}, s32[2,72,128]{2,1,0:T(8,128)}) custom-call(bf16[3,296,128]{2,1,0:T(8,128)(2,1)} %bitcast.11, bf16[8,296,296]{2,1,0:T(8,128)(2,1)} %m2m.1, s32[64,80]{1,0:T(8,128)} %bitcast.13, s32[64,80]{1,0:T(8,128)} %bitcast.14, s32[32,64]{1,0:T(8,128)} %bitcast.15, ...), custom_call_target="tpu_custom_call" | custom-call | tf_op jit(solution)/shard_map/exchange/pallas_call | solution.py:507
  15.2 24.2 %translate.1.partial = bf16[5,7,144,128]{3,2,1,0:T(8,128)(2,1)} custom-call(s32[2,72,128]{2,1,0:T(8,128)} %get-tuple-element.9.idx_in, bf16[3,296,128]{2,1,0:T(8,128)(2,1)} %bitcast.12, bf16[5,3,296,128]{3,2,1,0:T(8,128)(2,1)} %get-tuple-element.10.rem, bf16[5,7,16,128]{3,2,1,0:T(8,128)(2,1)} %get-tuple-element.11.par_in, bf16[64,296,296]{2,1,0:T(8,128)(2,1)} %ops_in.1), custom_call_target="tpu_custom_call" | custom-call | tf_op jit(solution)/shard_map/translate/pallas_call | solution.py:539
  39.4 14.1 %sums.1 = (f32[3,296,128]{2,1,0:T(8,128)}, f32[3,16,296]{2,1,0:T(8,128)}) custom-call(bf16[5,7,144,128]{3,2,1,0:T(8,128)(2,1)} %translate.1.partial), custom_call_target="tpu_custom_call" | custom-call | tf_op jit(solution)/shard_map/sums/pallas_call | solution.py:562
  53.4 17.2 %write.1 = (f32[3,296,128]{2,1,0:T(8,128)}, f32[3,16,296]{2,1,0:T(8,128)}) custom-call(f32[3,296,128]{2,1,0:T(8,128)} %get-tuple-element.12.leaf_in, f32[3,16,296]{2,1,0:T(8,128)} %get-tuple-element.13.parent_in), custom_call_target="tpu_custom_call" | custom-call | tf_op jit(solution)/shard_map/write/pallas_call | solution.py:585

commit v4 on v3

--- a/solution.py
+++ b/solution.py
@@ -110,11 +110,12 @@
             self.near.start()
             self.far.start()
 
+        self.sibling.start()
+
+    def start_unshared(self):
         @pl.when(self.in_ok)
         def _():
             self.behind.start()
-
-        self.sibling.start()
 
     def relay(self):
         @pl.when(self.out_ok)
@@ -249,6 +250,8 @@
     keep.start()
     parents = Spread(par_own, par, 4, psend, precv)
     parents.start()
+    parents.start_unshared()
+    leaves.start_unshared()
 
     leaf_base = (here() - 2) * BOX_DEV
     par_base = (here() - 2) * PAR_DEV - LEAVES
@@ -392,9 +395,8 @@
         put.wait()
 
 
-def sum_kernel(
-    partial, leaf, parent, own, mine_near, mine_far, from_near, from_far, side, behind, ahead,
-    send, recv, local,
+def return_kernel(
+    partial, side, behind, ahead, mine_near, mine_far, from_near, from_far, send, recv, local
 ):
     out, out_ok, in_ok = sides()
     first, rest = pl.ds(0, 4), pl.ds(4, 3)
@@ -402,7 +404,6 @@
         pltpu.make_async_copy(src, dst, local.at[n])
         for n, (src, dst) in enumerate(
             (
-                (partial.at[2], own),
                 (partial.at[2 + out, first], mine_near),
                 (partial.at[2 - 2 * out, rest], mine_far),
             )
@@ -462,46 +463,44 @@
         to_far.wait_recv()
         sum_far.wait_send()
 
-    @pl.when(jnp.logical_not(out_ok))
-    def _():
-        ahead[...] = jnp.zeros_like(ahead)
-
-    @pl.when(jnp.logical_not(in_ok))
-    def _():
-        behind[...] = jnp.zeros_like(behind)
+
+def sum_kernel(partial, side, behind, ahead, leaf, parent, got, leaf_sum, parent_sum, get, put):
+    gets = [
+        pltpu.make_async_copy(src, got.at[n], get.at[n])
+        for n, src in enumerate((partial.at[2], side, behind, ahead))
+    ]
+    for copy in gets:
+        copy.start()
+    _, out_ok, in_ok = sides()
+    for copy in gets:
+        copy.wait()
 
     def total(r):
-        s = own[r].astype(f32) + side[r].astype(f32)
-        return s + behind[r].astype(f32) + ahead[r].astype(f32)
-
+        s = got[0, r].astype(f32) + got[1, r].astype(f32)
+        s = s + jnp.where(in_ok, got[2, r].astype(f32), 0.0)
+        return s + jnp.where(out_ok, got[3, r].astype(f32), 0.0)
+
+    tails = total(6)
+    puts = []
     for c in range(3):
         for q in range(2):
             s = total(2 * c + q)
-            leaf[c, 128 * q : 128 * q + 128, :] = s[0:128]
-            parent[c, :, 128 * q : 128 * q + 128] = s[128:144]
-    s = total(6)
-    for c in range(3):
-        leaf[c, 256:296, :] = s[40 * c : 40 * c + 40]
-        shifted = s[128:144] if c == 0 else pltpu.roll(s[128:144], 128 - 40 * c, 1)
-        parent[c, :, 256:296] = shifted[:, :40]
-
-
-def write_kernel(leaf_in, parent_in, leaf, parent, sem):
-    copies = [
-        pltpu.make_async_copy(src.at[c], dst.at[c], sem.at[2 * c + n])
-        for c in range(3)
-        for n, (src, dst) in enumerate(((leaf_in, leaf), (parent_in, parent)))
-    ]
-    for copy in copies:
-        copy.start()
-    for copy in copies:
+            leaf_sum[c, 128 * q : 128 * q + 128, :] = s[0:128]
+            parent_sum[c, :, 128 * q : 128 * q + 128] = s[128:144]
+        leaf_sum[c, 256:296, :] = tails[40 * c : 40 * c + 40]
+        shifted = tails[128:144] if c == 0 else pltpu.roll(tails[128:144], 128 - 40 * c, 1)
+        parent_sum[c, :, 256:296] = shifted[:, :40]
+        puts.append(pltpu.make_async_copy(leaf_sum.at[c], leaf.at[c], put.at[c]))
+        puts[c].start()
+    puts.append(pltpu.make_async_copy(parent_sum, parent, put.at[3]))
+    puts[3].start()
+    for copy in puts:
         copy.wait()
 
 
 def on_device(multipole, m2m_ops, m2l_ops, lt, ls, pt, ps):
     mp = jnp.transpose(multipole, (1, 2, 0))
     pt, ps = jnp.transpose(pt[0]), jnp.transpose(ps[0])
-    vmem = pl.BlockSpec(memory_space=pltpu.VMEM)
     hbm = pl.BlockSpec(memory_space=pltpu.HBM)
     semaphores = pltpu.SemaphoreType.DMA
     rem, par, idx = pl.pallas_call(
@@ -559,38 +558,40 @@
         jax.ShapeDtypeStruct((3, P_SIZE, BOX_DEV), f32),
         jax.ShapeDtypeStruct((3, PAR_DEV, P_SIZE), f32),
     )
-    leaf, parent = pl.pallas_call(
-        sum_kernel,
-        out_shape=results,
+    side, behind, ahead = pl.pallas_call(
+        return_kernel,
+        out_shape=(jax.ShapeDtypeStruct(block, bf16),) * 3,
         in_specs=[hbm],
-        out_specs=(vmem, vmem),
+        out_specs=(hbm,) * 3,
         scratch_shapes=[
-            pltpu.VMEM(block, bf16),
             pltpu.VMEM((4,) + block[1:], bf16),
             pltpu.VMEM((3,) + block[1:], bf16),
             pltpu.VMEM((4,) + block[1:], bf16),
             pltpu.VMEM((3,) + block[1:], bf16),
-            pltpu.VMEM(block, bf16),
-            pltpu.VMEM(block, bf16),
-            pltpu.VMEM(block, bf16),
             semaphores((6,)),
             semaphores((6,)),
-            semaphores((3,)),
+            semaphores((2,)),
         ],
         compiler_params=pltpu.CompilerParams(
             collective_id=1, has_side_effects=True, vmem_limit_bytes=VMEM_BYTES
         ),
-        name="sums",
+        name="return",
     )(partial)
     leaf, parent = pl.pallas_call(
-        write_kernel,
+        sum_kernel,
         out_shape=results,
-        in_specs=[hbm, hbm],
+        in_specs=[hbm] * 4,
         out_specs=(hbm, hbm),
-        scratch_shapes=[semaphores((6,))],
+        scratch_shapes=[
+            pltpu.VMEM((4,) + block, bf16),
+            pltpu.VMEM((3, P_SIZE, BOX_DEV), f32),
+            pltpu.VMEM((3, PAR_DEV, P_SIZE), f32),
+            semaphores((4,)),
+            semaphores((4,)),
+        ],
         compiler_params=pltpu.CompilerParams(vmem_limit_bytes=VMEM_BYTES),
-        name="write",
-    )(leaf, parent)
+        name="sums",
+    )(partial, side, behind, ahead)
     return jnp.transpose(leaf, (2, 0, 1)), jnp.transpose(parent, (1, 0, 2))
 
 

time: 71 us -> 56.3 us (0.79)
  Pallas kernels: 70 us -> 55 us
    pallas_call x2, Pallas kernels: 31.2 us -> 15.5 us  [the longest x1 13.2 us: on_device(): pl.pallas_call(return_kernel, out_shape=(jax.ShapeDtypeStruct(block, bf16...]
where the time goes in v4:
time: 56.3 us; the launch traced here: 55.7 us
  Pallas kernels  55 us (98%)
  between operations  0.66 us (1%)
    pallas_call x1, Pallas kernels, on_device(): pl.pallas_call(translate_kernel, out_shape=jax.ShapeDtypeStruct((SPAN, 7,...  24.5 us
    pallas_call x1, Pallas kernels, on_device(): pl.pallas_call(exchange_kernel, out_shape=(jax.ShapeDtypeStruct((SPAN, 3,...  15 us
    pallas_call x1, Pallas kernels, on_device(): pl.pallas_call(return_kernel, out_shape=(jax.ShapeDtypeStruct(block, bf16...  13.2 us
    pallas_call x1, Pallas kernels, on_device(): pl.pallas_call(sum_kernel, out_shape=results, in_specs=[hbm] * 4, out_spe...  2.25 us

profile of v4, /device:TPU:31, one launch (start us, length us, event | category | flops | bytes accessed | tf_op | source)
XLA Modules:
  0.0 55.7 jit_solution(1743757353715739661)
XLA Ops:
  0.6 15.0 %exchange.1 = (bf16[5,3,296,128]{3,2,1,0:T(8,128)(2,1)}, bf16[5,7,16,128]{3,2,1,0:T(8,128)(2,1)}, s32[2,72,128]{2,1,0:T(8,128)}) custom-call(bf16[3,296,128]{2,1,0:T(8,128)(2,1)} %bitcast.11, bf16[8,296,296]{2,1,0:T(8,128)(2,1)} %m2m.1, s32[64,80]{1,0:T(8,128)} %bitcast.13, s32[64,80]{1,0:T(8,128)} %bitcast.14, s32[32,64]{1,0:T(8,128)} %bitcast.15, ...), custom_call_target="tpu_custom_call" | custom-call | tf_op jit(solution)/shard_map/exchange/pallas_call | solution.py:506
  15.6 24.5 %translate.1.partial = bf16[5,7,144,128]{3,2,1,0:T(8,128)(2,1)} custom-call(s32[2,72,128]{2,1,0:T(8,128)} %get-tuple-element.10.idx_in, bf16[3,296,128]{2,1,0:T(8,128)(2,1)} %bitcast.12, bf16[5,3,296,128]{3,2,1,0:T(8,128)(2,1)} %get-tuple-element.11.rem, bf16[5,7,16,128]{3,2,1,0:T(8,128)(2,1)} %get-tuple-element.12.par_in, bf16[64,296,296]{2,1,0:T(8,128)(2,1)} %ops_in.1), custom_call_target="tpu_custom_call" | custom-call | tf_op jit(solution)/shard_map/translate/pallas_call | solution.py:538
  40.2 13.2 %return.1 = (bf16[7,144,128]{2,1,0:T(8,128)(2,1)}, bf16[7,144,128]{2,1,0:T(8,128)(2,1)}, bf16[7,144,128]{2,1,0:T(8,128)(2,1)}) custom-call(bf16[5,7,144,128]{3,2,1,0:T(8,128)(2,1)} %translate.1.partial), custom_call_target="tpu_custom_call" | custom-call | tf_op jit(solution)/shard_map/return/pallas_call | solution.py:561
  53.4 2.2 %sums.1 = (f32[3,296,128]{2,1,0:T(8,128)}, f32[3,16,296]{2,1,0:T(8,128)}) custom-call(bf16[5,7,144,128]{3,2,1,0:T(8,128)(2,1)} %translate.1.partial, bf16[7,144,128]{2,1,0:T(8,128)(2,1)} %get-tuple-element.13.side, bf16[7,144,128]{2,1,0:T(8,128)(2,1)} %get-tuple-element.14.behind, bf16[7,144,128]{2,1,0:T(8,128)(2,1)} %get-tuple-element.15.ahead), custom_call_target="tpu_custom_call" | custom-call | tf_op jit(solution)/shard_map/sums/pallas_call | solution.py:580

commit v5 on v4

--- a/solution.py
+++ b/solution.py
@@ -11,6 +11,7 @@
 SLOT = 80
 PSLOT = 32
 BUCKETS = (3, 4, 5, 6, 7)
+STEP = 4
 SLOTS = SLOT + PSLOT
 P_SIZE = 296
 BOX_DEV = 128
@@ -110,12 +111,11 @@
             self.near.start()
             self.far.start()
 
-        self.sibling.start()
-
-    def start_unshared(self):
         @pl.when(self.in_ok)
         def _():
             self.behind.start()
+
+        self.sibling.start()
 
     def relay(self):
         @pl.when(self.out_ok)
@@ -207,8 +207,8 @@
     idx[0, 0:64, :] = jnp.where(lane == 120, order, source).astype(jnp.int32)
     idx[1, 0:64, :] = target.astype(jnp.int32)
     fits = mask16(count <= (16 * lane).astype(f32))
-    pairs = jnp.dot(ones[0:16, 0:64], fits, preferred_element_type=f32)[0:8]
-    idx[0, 64:72, :] = pairs.astype(jnp.int32) >> 1
+    groups = jnp.dot(ones[0:16, 0:64], fits, preferred_element_type=f32)[0:8]
+    idx[0, 64:72, :] = groups.astype(jnp.int32) // STEP
     idx[1, 64:72, :] = jnp.zeros((8, 128), jnp.int32)
 
 
@@ -250,8 +250,6 @@
     keep.start()
     parents = Spread(par_own, par, 4, psend, precv)
     parents.start()
-    parents.start_unshared()
-    leaves.start_unshared()
 
     leaf_base = (here() - 2) * BOX_DEV
     par_base = (here() - 2) * PAR_DEV - LEAVES
@@ -362,33 +360,35 @@
 
         @pl.when(end > start)
         def _():
-            gather(2 * start, 0, n)
+            gather(STEP * start, 0, n)
 
         @pl.loop(start, end)
         def _(i):
-            k = 2 * i
-            fetch(k).wait()
-            fetch(k + 1).wait()
-            gather(k + 1, 1, n)
-            multiply(k, 0, n)
-            scatter(jnp.maximum(k - 1, 0), 1, n)
-            gather(jnp.minimum(k + 2, CLASSES - 1), 0, n)
-            multiply(k + 1, 1, n)
-            scatter(k, 0, n)
+            first = STEP * i
+            for u in range(STEP):
+                fetch(first + u).wait()
+            for u in range(STEP):
+                k, now, other = first + u, u % 2, 1 - u % 2
+                gather(k + 1 if u < STEP - 1 else jnp.minimum(k + 1, CLASSES - 1), other, n)
+                multiply(k, now, n)
+                scatter(k - 1 if u else jnp.maximum(k - 1, 0), other, n)
 
         start = end
     scatter(CLASSES - 1, 1, SLOTS)
 
-    def total(first, count):
-        rows = pl.ds(first, count, stride=8)
-        return functools.reduce(lambda p, q: p + q, [a[rows, :] for a in acc])
+    def merge(first, count):
+        rows = pl.ds(first, count)
+        win[rows, :] = functools.reduce(lambda p, q: p + q, [a[rows, :] for a in acc])
 
     puts = []
     for j in range(SPAN):
+        leaf, parent = j * 1024, LEAVES * 8 + j * 128
+        merge(leaf, 1024)
+        merge(parent, 128)
         for r in range(7):
-            leaf = total(j * 1024 + r, 128).astype(bf16)
-            result[j, r, 0:128, :] = dot_nt(eye, leaf).astype(bf16)
-            result[j, r, 128:144, :] = total(LEAVES * 8 + j * 128 + r, 16).astype(bf16)
+            rows = win[pl.ds(leaf + r, 128, stride=8), :].astype(bf16)
+            result[j, r, 0:128, :] = dot_nt(eye, rows).astype(bf16)
+            result[j, r, 128:144, :] = win[pl.ds(parent + r, 16, stride=8), :].astype(bf16)
         puts.append(pltpu.make_async_copy(result.at[j], out.at[j], sem.at[7 + j]))
         puts[j].start()
     for put in puts:
@@ -465,24 +465,31 @@
 
 
 def sum_kernel(partial, side, behind, ahead, leaf, parent, got, leaf_sum, parent_sum, get, put):
+    pieces = (pl.ds(6, 1), pl.ds(0, 2), pl.ds(2, 2), pl.ds(4, 2))
     gets = [
-        pltpu.make_async_copy(src, got.at[n], get.at[n])
-        for n, src in enumerate((partial.at[2], side, behind, ahead))
+        [
+            pltpu.make_async_copy(src.at[rows], got.at[n, rows], get.at[4 * p + n])
+            for n, src in enumerate((partial.at[2], side, behind, ahead))
+        ]
+        for p, rows in enumerate(pieces)
     ]
-    for copy in gets:
-        copy.start()
+    for piece in gets:
+        for copy in piece:
+            copy.start()
     _, out_ok, in_ok = sides()
-    for copy in gets:
-        copy.wait()
 
     def total(r):
         s = got[0, r].astype(f32) + got[1, r].astype(f32)
         s = s + jnp.where(in_ok, got[2, r].astype(f32), 0.0)
         return s + jnp.where(out_ok, got[3, r].astype(f32), 0.0)
 
+    for copy in gets[0]:
+        copy.wait()
     tails = total(6)
     puts = []
     for c in range(3):
+        for copy in gets[1 + c]:
+            copy.wait()
         for q in range(2):
             s = total(2 * c + q)
             leaf_sum[c, 128 * q : 128 * q + 128, :] = s[0:128]
@@ -586,7 +593,7 @@
             pltpu.VMEM((4,) + block, bf16),
             pltpu.VMEM((3, P_SIZE, BOX_DEV), f32),
             pltpu.VMEM((3, PAR_DEV, P_SIZE), f32),
-            semaphores((4,)),
+            semaphores((16,)),
             semaphores((4,)),
         ],
         compiler_params=pltpu.CompilerParams(vmem_limit_bytes=VMEM_BYTES),

time: 56.3 us -> 54.4 us (0.966)
  Pallas kernels: 55 us -> 53.5 us
    pallas_call x1, Pallas kernels: 24.5 us -> 23.2 us  [on_device(): pl.pallas_call(translate_kernel, out_shape=jax.ShapeDtypeStruct((SPAN, 7,...]
where the time goes in v5:
time: 54.4 us; the launch traced here: 54.1 us
  Pallas kernels  53.5 us (98%)
  between operations  0.66 us (1%)
    pallas_call x1, Pallas kernels, on_device(): pl.pallas_call(translate_kernel, out_shape=jax.ShapeDtypeStruct((SPAN, 7,...  23.2 us
    pallas_call x1, Pallas kernels, on_device(): pl.pallas_call(exchange_kernel, out_shape=(jax.ShapeDtypeStruct((SPAN, 3,...  14.5 us
    pallas_call x1, Pallas kernels, on_device(): pl.pallas_call(return_kernel, out_shape=(jax.ShapeDtypeStruct(block, bf16...  13.5 us
    pallas_call x1, Pallas kernels, on_device(): pl.pallas_call(sum_kernel, out_shape=results, in_specs=[hbm] * 4, out_spe...  2.2 us

profile of v5, /device:TPU:31, one launch (start us, length us, event | category | flops | bytes accessed | tf_op | source)
XLA Modules:
  0.0 54.1 jit_solution(15103919123160728731)
XLA Ops:
  0.6 14.5 %exchange.1 = (bf16[5,3,296,128]{3,2,1,0:T(8,128)(2,1)}, bf16[5,7,16,128]{3,2,1,0:T(8,128)(2,1)}, s32[2,72,128]{2,1,0:T(8,128)}) custom-call(bf16[3,296,128]{2,1,0:T(8,128)(2,1)} %bitcast.11, bf16[8,296,296]{2,1,0:T(8,128)(2,1)} %m2m.1, s32[64,80]{1,0:T(8,128)} %bitcast.13, s32[64,80]{1,0:T(8,128)} %bitcast.14, s32[32,64]{1,0:T(8,128)} %bitcast.15, ...), custom_call_target="tpu_custom_call" | custom-call | tf_op jit(solution)/shard_map/exchange/pallas_call | solution.py:513
  15.2 23.2 %translate.1.partial = bf16[5,7,144,128]{3,2,1,0:T(8,128)(2,1)} custom-call(s32[2,72,128]{2,1,0:T(8,128)} %get-tuple-element.10.idx_in, bf16[3,296,128]{2,1,0:T(8,128)(2,1)} %bitcast.12, bf16[5,3,296,128]{3,2,1,0:T(8,128)(2,1)} %get-tuple-element.11.rem, bf16[5,7,16,128]{3,2,1,0:T(8,128)(2,1)} %get-tuple-element.12.par_in, bf16[64,296,296]{2,1,0:T(8,128)(2,1)} %ops_in.1), custom_call_target="tpu_custom_call" | custom-call | tf_op jit(solution)/shard_map/translate/pallas_call | solution.py:545
  38.4 13.5 %return.1 = (bf16[7,144,128]{2,1,0:T(8,128)(2,1)}, bf16[7,144,128]{2,1,0:T(8,128)(2,1)}, bf16[7,144,128]{2,1,0:T(8,128)(2,1)}) custom-call(bf16[5,7,144,128]{3,2,1,0:T(8,128)(2,1)} %translate.1.partial), custom_call_target="tpu_custom_call" | custom-call | tf_op jit(solution)/shard_map/return/pallas_call | solution.py:568
  51.9 2.2 %sums.1 = (f32[3,296,128]{2,1,0:T(8,128)}, f32[3,16,296]{2,1,0:T(8,128)}) custom-call(bf16[5,7,144,128]{3,2,1,0:T(8,128)(2,1)} %translate.1.partial, bf16[7,144,128]{2,1,0:T(8,128)(2,1)} %get-tuple-element.13.side, bf16[7,144,128]{2,1,0:T(8,128)(2,1)} %get-tuple-element.14.behind, bf16[7,144,128]{2,1,0:T(8,128)(2,1)} %get-tuple-element.15.ahead), custom_call_target="tpu_custom_call" | custom-call | tf_op jit(solution)/shard_map/sums/pallas_call | solution.py:587

commit v6 on v5

--- a/solution.py
+++ b/solution.py
@@ -57,25 +57,29 @@
     return out, (ahead >= 0) & (ahead < DEVICES), (behind >= 0) & (behind < DEVICES)
 
 
-def entry_barrier():
+def greet():
     barrier = pltpu.get_barrier_semaphore()
     out, out_ok, in_ok = sides()
 
-    def greet(offset):
+    def signal(offset):
         pl.semaphore_signal(barrier, inc=1, device_id=device_at(offset), device_id_type=MESH)
 
-    greet(-out)
+    signal(-out)
 
     @pl.when(out_ok)
     def _():
-        greet(out)
-        greet(2 * out)
+        signal(out)
+        signal(2 * out)
 
     @pl.when(in_ok)
     def _():
-        greet(-2 * out)
-
-    pl.semaphore_wait(barrier, 1 + 2 * out_ok.astype(jnp.int32) + in_ok.astype(jnp.int32))
+        signal(-2 * out)
+
+
+def await_greetings():
+    _, out_ok, in_ok = sides()
+    peers = 1 + 2 * out_ok.astype(jnp.int32) + in_ok.astype(jnp.int32)
+    pl.semaphore_wait(pltpu.get_barrier_semaphore(), peers)
 
 
 def remote(src, dst, send, recv, n, offset):
@@ -225,9 +229,7 @@
     ]
     for copy in staged:
         copy.start()
-    entry_barrier()
-    leaves = Spread(mp, rem, 2, send, recv)
-    leaves.start()
+    greet()
     for copy in staged:
         copy.wait()
 
@@ -246,10 +248,13 @@
         pieces.append(jnp.concatenate([part[:, 256:296], jnp.zeros((16, 88), f32)], axis=1))
     tails = pieces[0] + pltpu.roll(pieces[1], 40, 1) + pltpu.roll(pieces[2], 80, 1)
     par_own[6] = tails.astype(bf16)
+    await_greetings()
+    parents = Spread(par_own, par, 4, psend, precv)
+    leaves = Spread(mp, rem, 2, send, recv)
+    parents.start()
+    leaves.start()
     keep = pltpu.make_async_copy(par_own, par.at[2], local.at[6])
     keep.start()
-    parents = Spread(par_own, par, 4, psend, precv)
-    parents.start()
 
     leaf_base = (here() - 2) * BOX_DEV
     par_base = (here() - 2) * PAR_DEV - LEAVES
@@ -257,8 +262,8 @@
     put = pltpu.make_async_copy(idx, idx_out, local.at[7])
     put.start()
 
+    parents.relay()
     leaves.relay()
-    parents.relay()
     keep.wait()
     put.wait()
     leaves.finish()
@@ -418,7 +423,8 @@
     to_far = copy(partial.at[2 + 2 * out], behind, n=3, offset=2 * out)
     sum_near = copy(mine_near, ahead.at[first], n=4, offset=out)
     sum_far = copy(mine_far, ahead.at[rest], n=5, offset=-2 * out)
-    entry_barrier()
+    greet()
+    await_greetings()
 
     @pl.when(in_ok)
     def _():

time: 54.4 us -> 54.9 us (level)
    pallas_call x1, Pallas kernels: 13.5 us -> 14.1 us  [on_device(): pl.pallas_call(return_kernel, out_shape=(jax.ShapeDtypeStruct(block, bf16...]
where the time goes in v6:
time: 54.9 us; the launch traced here: 54.6 us
  Pallas kernels  53.9 us (98%)
  between operations  0.66 us (1%)
    pallas_call x1, Pallas kernels, on_device(): pl.pallas_call(translate_kernel, out_shape=jax.ShapeDtypeStruct((SPAN, 7,...  23.2 us
    pallas_call x1, Pallas kernels, on_device(): pl.pallas_call(exchange_kernel, out_shape=(jax.ShapeDtypeStruct((SPAN, 3,...  14.4 us
    pallas_call x1, Pallas kernels, on_device(): pl.pallas_call(return_kernel, out_shape=(jax.ShapeDtypeStruct(block, bf16...  14.1 us
    pallas_call x1, Pallas kernels, on_device(): pl.pallas_call(sum_kernel, out_shape=results, in_specs=[hbm] * 4, out_spe...  2.2 us

profile of v6, /device:TPU:31, one launch (start us, length us, event | category | flops | bytes accessed | tf_op | source)
XLA Modules:
  0.0 54.6 jit_solution(6754858151148729895)
XLA Ops:
  0.6 14.4 %exchange.1 = (bf16[5,3,296,128]{3,2,1,0:T(8,128)(2,1)}, bf16[5,7,16,128]{3,2,1,0:T(8,128)(2,1)}, s32[2,72,128]{2,1,0:T(8,128)}) custom-call(bf16[3,296,128]{2,1,0:T(8,128)(2,1)} %bitcast.11, bf16[8,296,296]{2,1,0:T(8,128)(2,1)} %m2m.1, s32[64,80]{1,0:T(8,128)} %bitcast.13, s32[64,80]{1,0:T(8,128)} %bitcast.14, s32[32,64]{1,0:T(8,128)} %bitcast.15, ...), custom_call_target="tpu_custom_call" | custom-call | tf_op jit(solution)/shard_map/exchange/pallas_call | solution.py:519
  15.0 23.2 %translate.1.partial = bf16[5,7,144,128]{3,2,1,0:T(8,128)(2,1)} custom-call(s32[2,72,128]{2,1,0:T(8,128)} %get-tuple-element.10.idx_in, bf16[3,296,128]{2,1,0:T(8,128)(2,1)} %bitcast.12, bf16[5,3,296,128]{3,2,1,0:T(8,128)(2,1)} %get-tuple-element.11.rem, bf16[5,7,16,128]{3,2,1,0:T(8,128)(2,1)} %get-tuple-element.12.par_in, bf16[64,296,296]{2,1,0:T(8,128)(2,1)} %ops_in.1), custom_call_target="tpu_custom_call" | custom-call | tf_op jit(solution)/shard_map/translate/pallas_call | solution.py:551
  38.3 14.1 %return.1 = (bf16[7,144,128]{2,1,0:T(8,128)(2,1)}, bf16[7,144,128]{2,1,0:T(8,128)(2,1)}, bf16[7,144,128]{2,1,0:T(8,128)(2,1)}) custom-call(bf16[5,7,144,128]{3,2,1,0:T(8,128)(2,1)} %translate.1.partial), custom_call_target="tpu_custom_call" | custom-call | tf_op jit(solution)/shard_map/return/pallas_call | solution.py:574
  52.4 2.2 %sums.1 = (f32[3,296,128]{2,1,0:T(8,128)}, f32[3,16,296]{2,1,0:T(8,128)}) custom-call(bf16[5,7,144,128]{3,2,1,0:T(8,128)(2,1)} %translate.1.partial, bf16[7,144,128]{2,1,0:T(8,128)(2,1)} %get-tuple-element.13.side, bf16[7,144,128]{2,1,0:T(8,128)(2,1)} %get-tuple-element.14.behind, bf16[7,144,128]{2,1,0:T(8,128)(2,1)} %get-tuple-element.15.ahead), custom_call_target="tpu_custom_call" | custom-call | tf_op jit(solution)/shard_map/sums/pallas_call | solution.py:593

commit v7 on v5

--- a/solution.py
+++ b/solution.py
@@ -248,8 +248,21 @@
     par_own[6] = tails.astype(bf16)
     keep = pltpu.make_async_copy(par_own, par.at[2], local.at[6])
     keep.start()
-    parents = Spread(par_own, par, 4, psend, precv)
-    parents.start()
+    out, out_ok, in_ok = sides()
+    to_side, to_near, to_far, to_behind = (
+        remote(par_own, par.at[2 - offset], psend, precv, n, offset)
+        for n, offset in enumerate((-out, out, 2 * out, -2 * out))
+    )
+    to_side.start()
+
+    @pl.when(out_ok)
+    def _():
+        to_near.start()
+        to_far.start()
+
+    @pl.when(in_ok)
+    def _():
+        to_behind.start()
 
     leaf_base = (here() - 2) * BOX_DEV
     par_base = (here() - 2) * PAR_DEV - LEAVES
@@ -258,11 +271,21 @@
     put.start()
 
     leaves.relay()
-    parents.relay()
     keep.wait()
     put.wait()
     leaves.finish()
-    parents.finish()
+    to_side.wait()
+
+    @pl.when(out_ok)
+    def _():
+        to_near.wait()
+        to_far.wait_send()
+        to_behind.wait_recv()
+
+    @pl.when(in_ok)
+    def _():
+        to_behind.wait_send()
+        to_far.wait_recv()
 
 
 def translate_kernel(
@@ -533,8 +556,8 @@
             pltpu.VMEM((2, 72, 128), jnp.int32),
             semaphores((6,)),
             semaphores((6,)),
-            semaphores((6,)),
-            semaphores((6,)),
+            semaphores((4,)),
+            semaphores((4,)),
             semaphores((8,)),
         ],
         compiler_params=pltpu.CompilerParams(

time: 54.4 us -> 54.7 us (level); the launches traced: 54.1 us -> 53.6 us
  Pallas kernels: 53.5 us -> 52.9 us
where the time goes in v7:
time: 54.7 us; the launch traced here: 53.6 us
  Pallas kernels  52.9 us (97%)
  between operations  0.66 us (1%)
    pallas_call x1, Pallas kernels, on_device(): pl.pallas_call(translate_kernel, out_shape=jax.ShapeDtypeStruct((SPAN, 7,...  23.2 us
    pallas_call x1, Pallas kernels, on_device(): pl.pallas_call(exchange_kernel, out_shape=(jax.ShapeDtypeStruct((SPAN, 3,...  14.3 us
    pallas_call x1, Pallas kernels, on_device(): pl.pallas_call(return_kernel, out_shape=(jax.ShapeDtypeStruct(block, bf16...  13.2 us
    pallas_call x1, Pallas kernels, on_device(): pl.pallas_call(sum_kernel, out_shape=results, in_specs=[hbm] * 4, out_spe...  2.2 us

profile of v7, /device:TPU:31, one launch (start us, length us, event | category | flops | bytes accessed | tf_op | source)
XLA Modules:
  0.0 53.6 jit_solution(7727307936828189358)
XLA Ops:
  0.6 14.3 %exchange.1 = (bf16[5,3,296,128]{3,2,1,0:T(8,128)(2,1)}, bf16[5,7,16,128]{3,2,1,0:T(8,128)(2,1)}, s32[2,72,128]{2,1,0:T(8,128)}) custom-call(bf16[3,296,128]{2,1,0:T(8,128)(2,1)} %bitcast.11, bf16[8,296,296]{2,1,0:T(8,128)(2,1)} %m2m.1, s32[64,80]{1,0:T(8,128)} %bitcast.13, s32[64,80]{1,0:T(8,128)} %bitcast.14, s32[32,64]{1,0:T(8,128)} %bitcast.15, ...), custom_call_target="tpu_custom_call" | custom-call | tf_op jit(solution)/shard_map/exchange/pallas_call | solution.py:536
  14.9 23.2 %translate.1.partial = bf16[5,7,144,128]{3,2,1,0:T(8,128)(2,1)} custom-call(s32[2,72,128]{2,1,0:T(8,128)} %get-tuple-element.10.idx_in, bf16[3,296,128]{2,1,0:T(8,128)(2,1)} %bitcast.12, bf16[5,3,296,128]{3,2,1,0:T(8,128)(2,1)} %get-tuple-element.11.rem, bf16[5,7,16,128]{3,2,1,0:T(8,128)(2,1)} %get-tuple-element.12.par_in, bf16[64,296,296]{2,1,0:T(8,128)(2,1)} %ops_in.1), custom_call_target="tpu_custom_call" | custom-call | tf_op jit(solution)/shard_map/translate/pallas_call | solution.py:568
  38.2 13.2 %return.1 = (bf16[7,144,128]{2,1,0:T(8,128)(2,1)}, bf16[7,144,128]{2,1,0:T(8,128)(2,1)}, bf16[7,144,128]{2,1,0:T(8,128)(2,1)}) custom-call(bf16[5,7,144,128]{3,2,1,0:T(8,128)(2,1)} %translate.1.partial), custom_call_target="tpu_custom_call" | custom-call | tf_op jit(solution)/shard_map/return/pallas_call | solution.py:591
  51.4 2.2 %sums.1 = (f32[3,296,128]{2,1,0:T(8,128)}, f32[3,16,296]{2,1,0:T(8,128)}) custom-call(bf16[5,7,144,128]{3,2,1,0:T(8,128)(2,1)} %translate.1.partial, bf16[7,144,128]{2,1,0:T(8,128)(2,1)} %get-tuple-element.13.side, bf16[7,144,128]{2,1,0:T(8,128)(2,1)} %get-tuple-element.14.behind, bf16[7,144,128]{2,1,0:T(8,128)(2,1)} %get-tuple-element.15.ahead), custom_call_target="tpu_custom_call" | custom-call | tf_op jit(solution)/shard_map/sums/pallas_call | solution.py:610

commit v8 on v7

--- a/solution.py
+++ b/solution.py
@@ -550,9 +550,9 @@
             pltpu.VMEM((CLASSES, SLOT), jnp.int32),
             pltpu.VMEM((PSLOT, CLASSES), jnp.int32),
             pltpu.VMEM((PSLOT, CLASSES), jnp.int32),
-            pltpu.VMEM((CLASSES * 8, 128), f32),
+            pltpu.VMEM((CLASSES * 8 + 8, 128), f32),
             pltpu.VMEM((CLASSES, 128), f32),
-            pltpu.VMEM((CLASSES * 8, 128), f32),
+            pltpu.VMEM((CLASSES * 8 + 8, 128), f32),
             pltpu.VMEM((2, 72, 128), jnp.int32),
             semaphores((6,)),
             semaphores((6,)),
@@ -575,9 +575,9 @@
             pltpu.VMEM((SPAN, 3, P_SIZE, BOX_DEV), bf16),
             pltpu.VMEM((SPAN, 7, PAR_DEV, 128), bf16),
             pltpu.VMEM((SPAN, 7, BOX_DEV + PAR_DEV, 128), bf16),
-            pltpu.VMEM((ROWS * 8, 128), f32),
+            pltpu.VMEM((ROWS * 8 + 8, 128), f32),
         ]
-        + [pltpu.VMEM((SLOTS * 8, 128), f32)] * 4
+        + [pltpu.VMEM((SLOTS * 8 + 8, 128), f32)] * 4
         + [pltpu.VMEM((CLASSES, P_SIZE, P_SIZE), bf16), semaphores((CLASSES,)), semaphores((12,))]
         + [pltpu.VMEM((ACC_ROWS * 8, 128), f32)] * CHAINS,
         compiler_params=pltpu.CompilerParams(vmem_limit_bytes=VMEM_BYTES),

time: 54.7 us -> 55 us (level); the launches traced: 53.6 us -> 54.7 us
  Pallas kernels: 52.9 us -> 54.1 us
    pallas_call x1, Pallas kernels: 23.2 us -> 23.9 us  [on_device(): pl.pallas_call(translate_kernel, out_shape=jax.ShapeDtypeStruct((SPAN, 7,...]
where the time goes in v8:
time: 55 us; the launch traced here: 54.7 us
  Pallas kernels  54.1 us (98%)
  between operations  0.66 us (1%)
    pallas_call x1, Pallas kernels, on_device(): pl.pallas_call(translate_kernel, out_shape=jax.ShapeDtypeStruct((SPAN, 7,...  23.9 us
    pallas_call x1, Pallas kernels, on_device(): pl.pallas_call(exchange_kernel, out_shape=(jax.ShapeDtypeStruct((SPAN, 3,...  14.3 us
    pallas_call x1, Pallas kernels, on_device(): pl.pallas_call(return_kernel, out_shape=(jax.ShapeDtypeStruct(block, bf16...  13.6 us
    pallas_call x1, Pallas kernels, on_device(): pl.pallas_call(sum_kernel, out_shape=results, in_specs=[hbm] * 4, out_spe...  2.2 us

profile of v8, /device:TPU:31, one launch (start us, length us, event | category | flops | bytes accessed | tf_op | source)
XLA Modules:
  0.0 54.7 jit_solution(6231359087210170290)
XLA Ops:
  0.6 14.3 %exchange.1 = (bf16[5,3,296,128]{3,2,1,0:T(8,128)(2,1)}, bf16[5,7,16,128]{3,2,1,0:T(8,128)(2,1)}, s32[2,72,128]{2,1,0:T(8,128)}) custom-call(bf16[3,296,128]{2,1,0:T(8,128)(2,1)} %bitcast.11, bf16[8,296,296]{2,1,0:T(8,128)(2,1)} %m2m.1, s32[64,80]{1,0:T(8,128)} %bitcast.13, s32[64,80]{1,0:T(8,128)} %bitcast.14, s32[32,64]{1,0:T(8,128)} %bitcast.15, ...), custom_call_target="tpu_custom_call" | custom-call | tf_op jit(solution)/shard_map/exchange/pallas_call | solution.py:536
  14.9 23.9 %translate.1.partial = bf16[5,7,144,128]{3,2,1,0:T(8,128)(2,1)} custom-call(s32[2,72,128]{2,1,0:T(8,128)} %get-tuple-element.10.idx_in, bf16[3,296,128]{2,1,0:T(8,128)(2,1)} %bitcast.12, bf16[5,3,296,128]{3,2,1,0:T(8,128)(2,1)} %get-tuple-element.11.rem, bf16[5,7,16,128]{3,2,1,0:T(8,128)(2,1)} %get-tuple-element.12.par_in, bf16[64,296,296]{2,1,0:T(8,128)(2,1)} %ops_in.1), custom_call_target="tpu_custom_call" | custom-call | tf_op jit(solution)/shard_map/translate/pallas_call | solution.py:568
  38.9 13.6 %return.1 = (bf16[7,144,128]{2,1,0:T(8,128)(2,1)}, bf16[7,144,128]{2,1,0:T(8,128)(2,1)}, bf16[7,144,128]{2,1,0:T(8,128)(2,1)}) custom-call(bf16[5,7,144,128]{3,2,1,0:T(8,128)(2,1)} %translate.1.partial), custom_call_target="tpu_custom_call" | custom-call | tf_op jit(solution)/shard_map/return/pallas_call | solution.py:591
  52.5 2.2 %sums.1 = (f32[3,296,128]{2,1,0:T(8,128)}, f32[3,16,296]{2,1,0:T(8,128)}) custom-call(bf16[5,7,144,128]{3,2,1,0:T(8,128)(2,1)} %translate.1.partial, bf16[7,144,128]{2,1,0:T(8,128)(2,1)} %get-tuple-element.13.side, bf16[7,144,128]{2,1,0:T(8,128)(2,1)} %get-tuple-element.14.behind, bf16[7,144,128]{2,1,0:T(8,128)(2,1)} %get-tuple-element.15.ahead), custom_call_target="tpu_custom_call" | custom-call | tf_op jit(solution)/shard_map/sums/pallas_call | solution.py:610
